TPU v7x, 32 devices: a whole 2x2x4 slice. The times are simulated.
32 devices in a mesh: lat: 8 (over z, y), lon: 4 (over x, core).
Axes of the slice: x: 2, y: 2, z: 4, core: 2. Of those that a mesh axis runs over, the one named last changes fastest.
Arguments:
- cube_cells: bfloat16 [1536, 80, 128], P(('lat', 'lon')), may hold values from -6 to 6
- block_source: int32 [720, 4, 4], P('lat', 'lon'), may hold values from 0 to 191, as said below
- block_weight: bfloat16 [720, 4, 4, 360, 128], P('lat', 'lon'), may hold values from -0.25 to 0.25
- lift_in: bfloat16 [80, 256], replicated, may hold values from -0.625 to 0.625
- lift_out: bfloat16 [256, 256], replicated, may hold values from -0.375 to 0.375
- spectral: bfloat16 [384, 256, 256], P('lon'), may hold values from -1.5 to 1.5
Outputs:
- grid_field: bfloat16 [720, 1440, 256], P('lat', 'lon')
Inputs may be any that keep to these rules, and one draw needn't show every extreme that they name: `block_source`: for target row r in band i = r // 90 and longitude block J, every entry is a position among band i's 192 tiles lying cyclically within 24 positions below or above the positions J * 48 to (J + 1) * 48 - 1. In the first row of every band and block, the first entry is the lowest position of that range and the second the highest.
All inputs are finite; a program needn't handle non-finite values.
Results may differ from a plain program's by a relative error of at most 0.015.
Values may be sent and summed in bfloat16 or wider, within the bound.
A program may use at most 320 MiB of HBM per device.

v0:
```python
import math

import jax
import jax.numpy as jnp
from jax import lax
from jax.sharding import PartitionSpec as P

NLAT = 720
NLON = 1440
L = 384
SRC_DEV = 48


unroll_steps = 16


def extended(cells, sides, width):
    for axis, dim in sides:
        count = lax.axis_size(axis)
        head = lax.slice_in_dim(cells, 0, width, axis=dim)
        tail = lax.slice_in_dim(cells, cells.shape[dim] - width, cells.shape[dim], axis=dim)
        cells = jnp.concatenate(
            [
                lax.ppermute(tail, axis, [(i, (i + 1) % count) for i in range(count)]),
                cells,
                lax.ppermute(head, axis, [((i + 1) % count, i) for i in range(count)]),
            ],
            axis=dim,
        )
    return cells


def legendre_setup(wave_orders):
    colatitude = (jnp.arange(NLAT, dtype=jnp.float32) + 0.5) * (math.pi / NLAT)
    cosine = jnp.cos(colatitude)[None, :]
    order_col = wave_orders.astype(jnp.float32)[:, None]
    log_scale = (
        0.5
        * (
            jnp.log(2.0 * order_col + 1.0)
            - math.log(4.0 * math.pi)
            + lax.lgamma(2.0 * order_col + 1.0)
            - 2.0 * lax.lgamma(order_col + 1.0)
            - order_col * math.log(4.0)
        )
        + order_col * jnp.log(jnp.sin(colatitude))[None, :]
    )
    initial = jnp.exp(jnp.minimum(log_scale + 80.0, 0.0))
    restore = jnp.exp(jnp.maximum(log_scale, -80.0))
    quadrature = jnp.sin(colatitude) * (math.pi / NLAT) * (2.0 * math.pi / NLON)
    return (cosine, order_col, initial, restore, quadrature)


def legendre_step(degree, current, earlier, cosine, order_col, initial):
    square = degree * degree
    rising = jnp.sqrt(
        jnp.maximum(4.0 * square - 1.0, 1.0) / jnp.maximum(square - order_col * order_col, 1.0)
    )
    shifted = (degree - 1.0) * (degree - 1.0)
    falling = jnp.sqrt(
        jnp.maximum(shifted - order_col * order_col, 0.0) / jnp.maximum(4.0 * shifted - 1.0, 1.0)
    )
    advanced = rising * (cosine * current - falling * earlier)
    return jnp.where(degree < order_col, 0.0, jnp.where(degree == order_col, initial, advanced))


def legendre_tables(wave_orders):
    cosine, order_col, initial, restore, quadrature = legendre_setup(wave_orders)

    def advance(carry, base_degree):
        current, earlier = carry
        stacked = []
        for offset in range(unroll_steps):
            latest = legendre_step(
                (base_degree + offset).astype(jnp.float32),
                current,
                earlier,
                cosine,
                order_col,
                initial,
            )
            earlier = current
            current = latest
            stacked.append(latest * restore)
        return ((current, earlier), jnp.stack(stacked))

    zeroed = jnp.zeros((wave_orders.shape[0], NLAT), jnp.float32)
    _, pieces = lax.scan(advance, (zeroed, zeroed), jnp.arange(0, L, unroll_steps, dtype=jnp.int32))
    table = pieces.reshape(L, wave_orders.shape[0], NLAT)
    return ((table * quadrature[None, None, :]).astype(jnp.bfloat16), table.astype(jnp.bfloat16))


def fourier_table(wave_orders):
    longitude = jnp.arange(NLON, dtype=jnp.int32)
    phase = longitude[:, None] * wave_orders[None, :] % NLON
    angle = phase.astype(jnp.float32) * (2.0 * math.pi / NLON)
    paired = jnp.stack([jnp.cos(angle), -jnp.sin(angle)], axis=2)
    return paired.reshape(NLON, 2 * wave_orders.shape[0])


def to_bands(values):
    return lax.all_to_all(values, "lat", split_axis=2, concat_axis=0, tiled=True)


def regroup(values):
    return lax.all_to_all(values, "lon", split_axis=3, concat_axis=1, tiled=True)


def analyse(table_part, data_part, first_block, block_width):
    order_count = table_part.shape[1]
    channel_count = data_part.shape[1]

    def fill_block(block_index, accumulated):
        table_block = lax.dynamic_slice_in_dim(
            table_part, block_index * block_width, block_width, 0
        )
        partial_value = jnp.einsum(
            "lmt,tcmp->mcpl", table_block, data_part, preferred_element_type=jnp.float32
        )
        return lax.dynamic_update_slice_in_dim(
            accumulated, partial_value, block_index * block_width, 3
        )

    zeroed = jnp.zeros((order_count, channel_count, 2, L), jnp.float32)
    return lax.fori_loop(first_block, L // block_width, fill_block, zeroed)


def synthesise(table_part, data_part, first_block, block_width):
    order_count = table_part.shape[1]
    channel_count = data_part.shape[3]

    def add_block(block_index, accumulated):
        table_block = lax.dynamic_slice_in_dim(
            table_part, block_index * block_width, block_width, 0
        )
        degree_rows = lax.dynamic_slice_in_dim(data_part, block_index * block_width, block_width, 1)
        return accumulated + jnp.einsum(
            "lmt,mlpd->mpdt", table_block, degree_rows, preferred_element_type=jnp.float32
        )

    zeroed = jnp.zeros((order_count, 2, channel_count, NLAT), jnp.float32)
    return lax.fori_loop(first_block, L // block_width, add_block, zeroed)


def shards(cube_cells, block_source, block_weight, lift_in, lift_out, spectral):
    lat_count = lax.axis_size("lat")
    lon_count = lax.axis_size("lon")
    lat_index = lax.axis_index("lat")
    lon_index = lax.axis_index("lon")
    block_width = min(128, L)
    rim_tiles = SRC_DEV // 2
    per_band = L // lat_count
    half_size = per_band // 2
    slot_index = jnp.arange(per_band, dtype=jnp.int32)[None, :]
    band_index = jnp.arange(lat_count, dtype=jnp.int32)[:, None]
    all_orders = band_index * per_band + slot_index
    column_orders = all_orders.reshape(lat_count * per_band)
    own_orders = lax.dynamic_index_in_dim(all_orders, lat_index, 0, keepdims=False)
    table_wide = fourier_table(column_orders)
    forward = table_wide.astype(jnp.bfloat16)
    widened = extended(cube_cells, (("lon", 0),), rim_tiles)
    band_tiles = lon_count * SRC_DEV
    offsets = (block_source[:, 0, :] - lon_index * SRC_DEV + rim_tiles) % band_tiles
    picked = widened[offsets]
    remapped = jnp.einsum(
        "rkts,rkcs->rtc", block_weight[:, 0], picked, preferred_element_type=jnp.float32
    ).astype(jnp.bfloat16)
    hidden = jax.nn.gelu(
        jnp.einsum("rtc,cd->rtd", remapped, lift_in, preferred_element_type=jnp.float32)
    ).astype(jnp.bfloat16)
    lifted = jnp.einsum("rtd,de->ret", hidden, lift_out, preferred_element_type=jnp.float32).astype(
        jnp.bfloat16
    )
    grid_rows = lax.all_to_all(lifted, "lon", split_axis=1, concat_axis=2, tiled=True)
    spectra = jnp.einsum(
        "rcl,lq->rcq", grid_rows, forward, preferred_element_type=jnp.float32
    ).astype(jnp.bfloat16)
    gathered = to_bands(spectra)
    channel_count = gathered.shape[1]
    gathered = gathered.reshape(NLAT, channel_count, per_band, 2)
    weighted, plain_table = legendre_tables(own_orders)
    sections = []
    for half_index in range(2):
        lowest = half_index * half_size
        first_block = own_orders[lowest] // block_width
        sections.append(
            analyse(
                weighted[:, lowest : lowest + half_size, :],
                gathered[:, :, lowest : lowest + half_size, :],
                first_block,
                block_width,
            )
        )
    analysis = jnp.concatenate(sections, axis=0).astype(jnp.bfloat16)
    by_degree = regroup(analysis)
    mixed_modes = jnp.einsum(
        "mcpl,lcd->mlpd", by_degree, spectral, preferred_element_type=jnp.float32
    ).astype(jnp.bfloat16)
    returned = regroup(mixed_modes)
    pieces = []
    for half_index in range(2):
        lowest = half_index * half_size
        first_block = own_orders[lowest] // block_width
        pieces.append(
            synthesise(
                plain_table[:, lowest : lowest + half_size, :],
                returned[lowest : lowest + half_size],
                first_block,
                block_width,
            )
        )
    synthesized = (
        jnp.concatenate(pieces, axis=0)
        .astype(jnp.bfloat16)
        .reshape(2 * per_band, channel_count, NLAT)
    )
    rows_back = to_bands(synthesized)
    factors = jnp.repeat(jnp.where(column_orders == 0, 1.0, 2.0), 2).astype(jnp.bfloat16)
    inverse = forward * factors[None, :]
    grid_field = jnp.einsum(
        "qcr,kq->rkc", rows_back, inverse, preferred_element_type=jnp.float32
    ).astype(jnp.bfloat16)
    return lax.all_to_all(grid_field, "lon", split_axis=1, concat_axis=2, tiled=True)


def solution(mesh):
    in_specs = (
        P(("lat", "lon"), None, None),
        P("lat", "lon", None),
        P("lat", "lon", None, None, None),
        P(),
        P(),
        P("lon", None, None),
    )
    out_specs = P("lat", "lon", None)
    return jax.shard_map(shards, mesh=mesh, in_specs=in_specs, out_specs=out_specs, check_vma=False)
```

profile of v0, /device:TPU:0, one launch (start us, length us, event | category | flops | bytes accessed | tf_op | source)
XLA Modules:
  0.0 2103.1 jit_solution(15478067676584799692)
XLA Ops:
  4.7 8.1 collective-permute-done
  16.7 14.2 gather_fusion
  30.9 18.9 fusion.92
  49.9 21.7 %convert_bitcast_fusion.1 = bf16[90,256,360]{1,2,0:T(8,128)(2,1)} fusion(bf16[90,80,360,1]{2,1,3,0:T(8,128)(2,1)} %fusion.92, bf16[256,256]{1,0:T(8,128)(2,1)S(1)} %copy-done, bf16[80,256]{1,0:T(8,128)(2,1)S(1)} %copy-done.5), kind=kOutput, calls=%fused_computation.175 | convolution fusion | flops 5656780800 | bytes 21944832 | tf_op jit(solution)/shard_map/rtd,de->ret/dot_general | solution.py:171
  71.6 23.9 %copy.130 = bf16[90,256,360]{2,0,1:T(8,128)(2,1)} copy(bf16[90,256,360]{1,2,0:T(8,128)(2,1)} %convert_bitcast_fusion.1) | data formatting | bytes 33177600 | tf_op jit(solution)/shard_map/convert_element_type | solution.py:171
  95.5 7.3 all-to-all-start
  103.1 9.5 cosine_convert_fusion
  115.1 5.9 copy.133
  124.0 184.7 %all-to-all-done = bf16[90,256,360]{2,0,1:T(8,128)(2,1)} async-done(((bf16[90,256,360]{2,0,1:T(8,128)(2,1)}), bf16[90,256,360]{2,0,1:T(8,128)(2,1)}, u32[]{:S(2)}, u32[]{:S(2)}) %all-to-all-start) | async-done | bytes 16588832 | tf_op jit(solution)/shard_map/all_to_all | solution.py:174
  308.8 23.3 %copy.132 = bf16[90,64,4,360]{3,2,1,0:T(4,128)(2,1)} copy(bf16[90,64,4,360]{3,0,1,2:T(8,128)(2,1)} %bitcast.26) | data formatting | bytes 33177600 | tf_op jit(solution)/shard_map/all_to_all | solution.py:174
  332.1 30.9 %all_to_all.77 = bf16[90,64,1440]{2,1,0:T(8,128)(2,1)} reshape(bf16[90,64,4,360]{3,2,1,0:T(4,128)(2,1)} %copy.132) | data formatting | bytes 33177600 | tf_op jit(solution)/shard_map/all_to_all | solution.py:174
  363.0 20.3 convolution_convert_fusion
  383.3 17.1 copy.135
  400.3 5.8 all-to-all-start.1
  406.2 376.9 %while.65 = (s32[]{:T(128)}, f32[48,720]{1,0:T(8,128)S(1)}, f32[48,720]{1,0:T(8,128)S(1)}, f32[24,16,48,720]{3,2,1,0:T(8,128)}, s32[24]{0:T(128)S(1)}, /*index=5...) while((s32[]{:T(128)}, f32[48,720]{1,0:T(8,128)S(1)}, ...), condition=%wide.region_1.2_spmd.clone.clone.clone.clone, body=%wide.region_0.1_spmd.clone.clone.clone.clone.sunk | while | flops 6746961 | bytes 14180144 | solution.py:88
  788.7 53.9 %copy.128 = f32[384,48,720]{0,2,1:T(8,128)} copy(f32[384,48,720]{2,1,0:T(8,128)} %bitcast.416) | data formatting | bytes 106168320 | tf_op jit(solution)/shard_map/reshape | solution.py:89
  842.6 51.0 %fusion.148 = (bf16[384,48,720]{0,2,1:T(8,128)(2,1)}, bf16[384,48,720]{0,2,1:T(8,128)(2,1)}) fusion(f32[384,48,720]{0,2,1:T(8,128)} %copy.128, f32[720]{0:T(1024)S(1)} %fusion.117), kind=kLoop, calls=%fused_computation.261 | loop fusion | flops 39813120 | bytes 106171200 | tf_op jit(solution)/shard_map/convert_element_type | solution.py:90
  893.6 36.1 %fusion.149 = (bf16[384,24,720]{0,2,1:T(8,128)(2,1)}, bf16[384,24,720]{0,2,1:T(8,128)(2,1)}, bf16[384,24,720]{0,2,1:T(8,128)(2,1)}, bf16[384,24,720]{0,2,1:T(8,128)(2,1)}) fusion(bf16[384,48,720]{0,2,1:T(8,128)(2,1)} %get-tuple-element.667, bf16[384,48,720]{0,2,1:T(8,128)(2,1)} %get-tuple-element.668), kind=kLoop, calls=%fused_computation.262 | loop fusion | bytes 106168320 | tf_op jit(solution)/shard_map/slice | solution.py:206
  929.7 15.8 copy.172
  945.5 19.9 reshape.1451
  965.4 8.7 fusion.151
  974.5 16.3 while.61
  974.5 5.4 bitcast_dynamic-update-slice_fusion.38
  979.9 5.4 bitcast_dynamic-update-slice_fusion.38
  985.3 5.4 bitcast_dynamic-update-slice_fusion.38
  990.8 8.6 copy.137
  999.7 16.5 while.62
  999.7 5.4 bitcast_dynamic-update-slice_fusion.39
  1005.2 5.4 bitcast_dynamic-update-slice_fusion.39
  1010.6 5.4 bitcast_dynamic-update-slice_fusion.39
  1016.2 8.6 copy.138
  1024.8 46.4 %fusion.155 = bf16[384,48,2,64]{3,2,1,0:T(2,128)(2,1)} fusion(bf16[24,64,2,384]{1,2,0,3:T(2,128)(2,1)} %copy.138, bf16[24,64,2,384]{1,2,0,3:T(2,128)(2,1)} %copy.137), kind=kLoop, calls=%fused_computation.268 | loop fusion | flops 2359296 | bytes 9437184
  1071.2 10.4 reshape.1473
  1081.5 59.8 %all_to_all.102 = bf16[4,2,294912]{2,1,0:T(2,128)(2,1)} all-to-all(bf16[4,2,294912]{2,1,0:T(2,128)(2,1)} %reshape.1473), channel_id=1, replica_groups=mesh['lat'=8,'lon'=4] {'lon'}, dimensions={0} | all-to-all | bytes 9437184 | tf_op jit(solution)/shard_map/all_to_all | solution.py:106
  1141.3 10.2 reshape.1474
  1151.5 21.4 %copy.139 = bf16[48,64,2,4,96]{4,1,3,2,0:T(8,128)(2,1)} copy(bf16[48,64,2,4,96]{1,2,0,4,3:T(2,128)(2,1)} %bitcast.419) | data formatting | bytes 9437184 | tf_op jit(solution)/shard_map/all_to_all | solution.py:106
  1172.9 8.4 copy.140
  1181.3 10.3 convert_bitcast_fusion.2
  1191.7 9.1 copy.141
  1200.8 75.0 %all_to_all.103 = bf16[48,96,2,256]{1,0,2,3:T(8,128)(2,1)S(1)} all-to-all(bf16[48,96,2,256]{1,0,2,3:T(8,128)(2,1)} %copy.141), channel_id=1, replica_groups=mesh['lat'=8,'lon'=4] {'lon'}, dimensions={3} | all-to-all | bytes 9437184 | tf_op jit(solution)/shard_map/all_to_all | solution.py:106
  1286.0 5.0 slice.55
  1295.8 31.4 %while.63 = (s32[]{:T(128)}, f32[24,2,64,720]{3,2,1,0:T(8,128)}, bf16[24,384,2,64]{1,3,2,0:T(8,128)(2,1)S(1)}, bf16[384,24,720]{0,2,1:T(8,128)(2,1)}, s32[]{:T(128)}, /*index=5*/s32[]{:T(128)}, s32[]{:T(128)}, s32[]{:T(128)}) while((s32[]{:T(128)}, f32[24,2,64,720]{3,2,1,0:T(8,128)}, bf16[24,384,2,64]{1,3,2,0:T(8,128)(2,1)S(1)}, ...), condition=%wide.region_7.8_spmd, body=%wide.region_6.7_spmd.sunk | while | flops 568442880 | bytes 23495812 | solution.py:142
  1295.8 10.4 fusion.178
  1306.2 10.4 fusion.178
  1316.6 10.4 fusion.178
  1327.2 6.7 convert.22
  1338.6 5.0 slice.58
  1348.5 31.5 %while.64 = (s32[]{:T(128)}, f32[24,2,64,720]{3,2,1,0:T(8,128)}, bf16[24,384,2,64]{1,3,2,0:T(8,128)(2,1)S(1)}, bf16[384,24,720]{0,2,1:T(8,128)(2,1)}, s32[]{:T(128)}, /*index=5*/s32[]{:T(128)}, s32[]{:T(128)}, s32[]{:T(128)}) while((s32[]{:T(128)}, f32[24,2,64,720]{3,2,1,0:T(8,128)}, bf16[24,384,2,64]{1,3,2,0:T(8,128)(2,1)S(1)}, ...), condition=%wide.region_9.10_spmd, body=%wide.region_8.9_spmd.sunk | while | flops 568442880 | bytes 23495812 | solution.py:142
  1348.5 10.5 fusion.181
  1359.0 10.5 fusion.181
  1369.5 10.5 fusion.181
  1384.4 6.6 pad_maximum_fusion.1
  1391.0 17.2 copy.146
  1408.2 5.5 all-to-all-start.4
  1413.7 5.9 copy.127
  1422.6 247.2 %all-to-all-done.4 = bf16[96,64,720]{0,1,2:T(8,128)(2,1)} async-done(((bf16[96,64,720]{0,1,2:T(8,128)(2,1)}), bf16[96,64,720]{0,1,2:T(8,128)(2,1)}, u32[]{:S(2)}, u32[]{:S(2)}) %all-to-all-start.4) | async-done | bytes 8847392 | tf_op jit(solution)/shard_map/all_to_all | solution.py:102
  1669.7 13.9 copy.168
  1683.6 18.4 reshape.1471
  1702.0 21.1 %convert_bitcast_fusion = bf16[90,1440,64]{1,0,2:T(8,128)(2,1)} fusion(bf16[768,64,90]{0,2,1:T(8,128)(2,1)} %reshape.1471, bf16[1440,768]{0,1:T(8,128)(2,1)S(1)} %copy-done.4), kind=kOutput, calls=%fused_computation.174 | convolution fusion | flops 12748492800 | bytes 27648000 | tf_op jit(solution)/shard_map/qcr,kq->rkc/dot_general | solution.py:220
  1723.1 30.9 %copy.151 = bf16[90,1440,64]{0,2,1:T(8,128)(2,1)} copy(bf16[90,1440,64]{1,0,2:T(8,128)(2,1)} %convert_bitcast_fusion) | data formatting | bytes 33177600 | tf_op jit(solution)/shard_map/convert_element_type | solution.py:222
  1754.0 270.0 %all_to_all.104 = bf16[90,1440,64]{0,2,1:T(8,128)(2,1)} all-to-all(bf16[90,1440,64]{0,2,1:T(8,128)(2,1)} %copy.151), channel_id=1, replica_groups=mesh['lat'=8,'lon'=4] {'lon'}, dimensions={1} | all-to-all | bytes 33177600 | tf_op jit(solution)/shard_map/all_to_all | solution.py:223
  2024.0 38.2 %copy.169 = bf16[90,4,360,64]{2,1,3,0:T(4,128)(2,1)} copy(bf16[90,4,360,64]{0,3,2,1:T(8,128)(2,1)} %bitcast.413) | data formatting | bytes 33177600 | tf_op jit(solution)/shard_map/all_to_all | solution.py:223
  2062.2 17.3 copy.153
  2079.5 23.4 %copy.154 = bf16[90,360,256]{2,1,0:T(8,128)(2,1)} copy(bf16[90,360,256]{1,2,0:T(8,128)(2,1)} %bitcast.415) | data formatting | bytes 33177600 | tf_op jit(solution)/shard_map/all_to_all | solution.py:223
  (624 shorter events, 167.2 us)
Async XLA Ops:
  0.0 49.9 %copy-start = (bf16[256,256]{1,0:T(8,128)(2,1)S(1)}, bf16[256,256]{1,0:T(8,128)(2,1)}, u32[]{:S(2)}) copy-start(bf16[256,256]{1,0:T(8,128)(2,1)} %param.20) | copy-start | bytes 393220
  1.3 11.5 collective-permute-start
  1.8 13.5 collective-permute-start.1
  30.9 19.0 copy-start.5
  95.5 213.2 %all-to-all-start = ((bf16[90,256,360]{2,0,1:T(8,128)(2,1)}), bf16[90,256,360]{2,0,1:T(8,128)(2,1)}, u32[]{:S(2)}, u32[]{:S(2)}) async-start(bf16[90,256,360]{2,0,1:T(8,128)(2,1)} %copy.130), calls=%async_computation | async-start | bytes 37748736 | tf_op jit(solution)/shard_map/all_to_all | solution.py:174
  332.1 30.9 %copy-start.3 = (bf16[1440,768]{0,1:T(8,128)(2,1)S(1)}, bf16[1440,768]{0,1:T(8,128)(2,1)}, u32[]{:S(2)}) copy-start(bf16[1440,768]{0,1:T(8,128)(2,1)} %convert_element_type.277) | copy-start | bytes 6635524
  400.3 529.4 %all-to-all-start.1 = ((bf16[90,64,768]{0,1,2:T(8,128)(2,1)}), bf16[90,64,768]{0,1,2:T(8,128)(2,1)}, u32[]{:S(2)}, u32[]{:S(2)}) async-start(bf16[90,64,768]{0,1,2:T(8,128)(2,1)} %copy.135), calls=%async_computation.1 | async-start | bytes 25165824 | tf_op jit(solution)/shard_map/all_to_all | solution.py:102
  1327.2 6.7 copy-start.2
  1408.2 261.5 %all-to-all-start.4 = ((bf16[96,64,720]{0,1,2:T(8,128)(2,1)}), bf16[96,64,720]{0,1,2:T(8,128)(2,1)}, u32[]{:S(2)}, u32[]{:S(2)}) async-start(bf16[96,64,720]{0,1,2:T(8,128)(2,1)} %copy.146), calls=%async_computation.4 | async-start | bytes 23592960 | tf_op jit(solution)/shard_map/all_to_all | solution.py:102
  1683.6 18.4 copy-start.4
  2079.5 23.4 %copy-start.1 = (bf16[256,256]{1,0:T(8,128)(2,1)S(1)}, bf16[256,256]{1,0:T(8,128)(2,1)}, u32[]{:S(2)}) copy-start(bf16[256,256]{1,0:T(8,128)(2,1)} %param.20) | copy-start | bytes 393220
where the time goes:
time: 2120 us; the launch traced here: 2100 us
  local copies, waits for them, and re-layouts  587 us (28%)
  waiting for transfers between devices  442 us (21%)
  blocking collectives  405 us (19%)
  loops' own time  258 us (12%)
  other arithmetic  197 us (9%)
  matrix products  188 us (9%)
  starting transfers between devices  21.2 us (1%)
    all_to_all x1, blocking collectives, shards(): lax.all_to_all(grid_field, 'lon', split_axis=1, concat_axis=2, tiled=True)  270 us
    another operation x1, loops' own time, legendre_tables(): lax.scan(advance, (zeroed, zeroed), jnp.arange(0, L, unroll_steps, dtype=...  257 us
    all_to_all x2, waiting for transfers between devices, to_bands(): lax.all_to_all(values, 'lat', split_axis=2, concat_axis=0, tiled=True)  247 us
    all_to_all x1, waiting for transfers between devices, shards(): lax.all_to_all(lifted, 'lon', split_axis=1, concat_axis=2, tiled=True)  185 us
    all_to_all x2, blocking collectives, regroup(): lax.all_to_all(values, 'lon', split_axis=3, concat_axis=1, tiled=True)  135 us
    all_to_all x3, local copies, waits for them, and re-layouts, shards(): lax.all_to_all(grid_field, 'lon', split_axis=1, concat_axis=2, tiled=True)  78.9 us
    dot_general x6, matrix products, add_block(): jnp.einsum('lmt,mlpd->mpdt', table_block, degree_rows, preferred_element_...  62.8 us
    while x360, other arithmetic  56.9 us
  transfers between devices with their start and end apart: 5, of which 4 were waited for; matrix products, arithmetic and copies ran while one was open for 14% of the time, Pallas kernels for 0%

commit v1 on v0

--- a/solution.py
+++ b/solution.py
@@ -3,6 +3,8 @@
 import jax
 import jax.numpy as jnp
 from jax import lax
+from jax.experimental import pallas as pl
+from jax.experimental.pallas import tpu as pltpu
 from jax.sharding import PartitionSpec as P
 
 NLAT = 720
@@ -223,7 +225,361 @@
     return lax.all_to_all(grid_field, "lon", split_axis=1, concat_axis=2, tiled=True)
 
 
+PARTS = 3
+PAIRS = 3
+STEP = 16
+F32 = jnp.float32
+BF16 = jnp.bfloat16
+
+
+def params():
+    return pltpu.CompilerParams(vmem_limit_bytes=56 * 1024 * 1024)
+
+
+def cost(flops, moved):
+    return pl.CostEstimate(flops=flops, bytes_accessed=moved, transcendentals=0)
+
+
+def whole_block(shape):
+    zeros = (0,) * len(shape)
+    return pl.BlockSpec(shape, lambda *_: zeros)
+
+
+def halves(left, right, at):
+    return jnp.concatenate([left[:, at : at + 64], right[:, at : at + 64]], axis=1)
+
+
+def lift_kernel(first_row, picks, tiles, weight, lift_in, lift_out, out):
+    rows = []
+    for r in range(2):
+        row = first_row + pl.program_id(0) * 2 + r
+        source = jnp.concatenate([tiles[picks[row * 4 + k]] for k in range(4)], axis=1)
+        blocks = jnp.concatenate([weight[r, k] for k in range(4)], axis=1)
+        remapped = lax.dot_general(
+            blocks, source, (((1,), (1,)), ((), ())), preferred_element_type=F32
+        ).astype(BF16)
+        hidden = jax.nn.gelu(jnp.dot(remapped, lift_in[...], preferred_element_type=F32))
+        rows.append(
+            jnp.dot(hidden.astype(BF16), lift_out[...], preferred_element_type=F32).astype(BF16)
+        )
+    for q in range(4):
+        out[q, 0] = halves(rows[0], rows[1], 64 * q)
+
+
+def lift_part(part, pairs, picks, tiles, weight, lift_in, lift_out):
+    width = weight.shape[2]
+    return pl.pallas_call(
+        lambda *refs: lift_kernel(part * pairs * 2, *refs),
+        out_shape=jax.ShapeDtypeStruct((4, pairs, width, 128), BF16),
+        grid_spec=pltpu.PrefetchScalarGridSpec(
+            num_scalar_prefetch=1,
+            grid=(pairs,),
+            in_specs=[
+                whole_block(tiles.shape),
+                pl.BlockSpec((2, 4, width, 128), lambda g, _: (part * pairs + g, 0, 0, 0)),
+                whole_block(lift_in.shape),
+                whole_block(lift_out.shape),
+            ],
+            out_specs=pl.BlockSpec((4, 1, width, 128), lambda g, _: (0, g, 0, 0)),
+        ),
+        compiler_params=params(),
+        cost_estimate=cost(pairs * 2 * width * 256 * 256 * 4, pairs * width * 128 * 24),
+        name="lift_rows",
+    )(picks, tiles, weight, lift_in, lift_out)
+
+
+def dft_kernel(table, data, scale, out):
+    total = None
+    for j in range(4):
+        block = jnp.concatenate([data[j, g] for g in range(PAIRS)], axis=1)
+        term = jnp.dot(table[j], block, preferred_element_type=F32)
+        total = term if total is None else total + term
+    total = total * scale[0]
+    half = total.shape[0] // 2
+    orders = half // 8
+    for r in range(2 * PAIRS):
+        row = halves(total[:half], total[half:], 64 * r).astype(BF16)
+        for i in range(8):
+            out[i, r] = row[i * orders : (i + 1) * orders]
+
+
+def dft_part(table, data, scale):
+    _, pairs, width, _ = data.shape
+    waves = table.shape[1]
+    rows = 2 * PAIRS
+    return pl.pallas_call(
+        dft_kernel,
+        out_shape=jax.ShapeDtypeStruct((8, 2 * pairs, waves // 16, 128), BF16),
+        grid=(pairs // PAIRS,),
+        in_specs=[
+            whole_block(table.shape),
+            pl.BlockSpec((4, PAIRS, width, 128), lambda g: (0, g, 0, 0)),
+            pl.BlockSpec((1, 1, 64 * rows), lambda g: (g, 0, 0)),
+        ],
+        out_specs=pl.BlockSpec((8, rows, waves // 16, 128), lambda g: (0, g, 0, 0)),
+        compiler_params=params(),
+        cost_estimate=cost(pairs * 128 * 4 * width * waves * 2, pairs * 128 * 4 * width * 4),
+        name="forward_rows",
+    )(table, data, scale)
+
+
+def legendre_kernel(cosine, order, initial, restore, out, current, earlier, held):
+    base = pl.program_id(0) * STEP
+
+    @pl.when(base == 0)
+    def _():
+        current[...] = jnp.zeros_like(current)
+        earlier[...] = jnp.zeros_like(earlier)
+
+    orders = order.shape[0]
+    now, before = current[...], earlier[...]
+    for s in range(STEP):
+        degree = (base + s).astype(F32)
+        square = degree * degree
+        order_square = order[...] * order[...]
+        rising = jnp.sqrt(
+            jnp.maximum(4.0 * square - 1.0, 1.0) / jnp.maximum(square - order_square, 1.0)
+        )
+        shifted = (degree - 1.0) * (degree - 1.0)
+        falling = jnp.sqrt(
+            jnp.maximum(shifted - order_square, 0.0) / jnp.maximum(4.0 * shifted - 1.0, 1.0)
+        )
+        advanced = rising * (cosine[...] * now - falling * before)
+        latest = jnp.where(
+            degree < order[...], 0.0, jnp.where(degree == order[...], initial[...], advanced)
+        )
+        now, before = latest, now
+        held[s] = latest * restore[...]
+    current[...] = now
+    earlier[...] = before
+    out[...] = jnp.swapaxes(held[...], 0, 1)[:, :, : out.shape[2]].astype(BF16)
+
+
+def legendre_table(orders, row_order):
+    cosine, order_col, initial, restore, quadrature = legendre_setup(orders)
+    extra = ((0, 0), (0, -NLAT % 128))
+    cosine, initial, restore = (
+        jnp.pad(value[:, row_order], extra) for value in (cosine, initial, restore)
+    )
+    count, wide = initial.shape
+    table = pl.pallas_call(
+        legendre_kernel,
+        out_shape=jax.ShapeDtypeStruct((count, L, NLAT), BF16),
+        grid=(L // STEP,),
+        in_specs=[
+            whole_block((1, wide)),
+            whole_block((count, 1)),
+            whole_block((count, wide)),
+            whole_block((count, wide)),
+        ],
+        out_specs=pl.BlockSpec((count, STEP, NLAT), lambda g: (0, g, 0)),
+        scratch_shapes=[
+            pltpu.VMEM((count, wide), F32),
+            pltpu.VMEM((count, wide), F32),
+            pltpu.VMEM((STEP, count, wide), F32),
+        ],
+        compiler_params=params(),
+        cost_estimate=cost(L * count * wide * 100, count * L * NLAT * 2),
+        name="legendre_table",
+    )(cosine, order_col, initial, restore)
+    return table, quadrature
+
+
+def analysis_kernel(table, first, second, third, out):
+    for m in range(table.shape[0]):
+        rows = jnp.concatenate([first[m], second[m], third[m]], axis=0)
+        out[m] = jnp.dot(table[m], rows, preferred_element_type=F32).astype(BF16)
+
+
+def analysis_all(table, pieces, group=4):
+    count = table.shape[0]
+    depth = pieces[0].shape[1]
+    return pl.pallas_call(
+        analysis_kernel,
+        out_shape=jax.ShapeDtypeStruct((count, L, 128), BF16),
+        grid=(count // group,),
+        in_specs=[pl.BlockSpec((group, L, NLAT), lambda g: (g, 0, 0))]
+        + [pl.BlockSpec((group, depth, 128), lambda g: (g, 0, 0))] * 3,
+        out_specs=pl.BlockSpec((group, L, 128), lambda g: (g, 0, 0)),
+        compiler_params=params(),
+        cost_estimate=cost(count * L * NLAT * 256, count * L * NLAT * 2),
+        name="analysis",
+    )(table, *pieces)
+
+
+def mix_kernel(data, matrix, out):
+    for l in range(data.shape[1]):
+        sides = []
+        for p in range(2):
+            sides.append(
+                jnp.concatenate([data[j, l][:, 64 * p : 64 * p + 64] for j in range(4)], axis=1)
+            )
+        joined = jnp.concatenate(sides, axis=0)
+        mixed = jnp.dot(joined, matrix[l], preferred_element_type=F32).astype(BF16)
+        count = data.shape[2]
+        for q in range(4):
+            out[q, l] = halves(mixed[:count], mixed[count:], 64 * q)
+
+
+def mix_all(data, matrix, group=8):
+    _, degrees, count, _ = data.shape
+    spec = pl.BlockSpec((4, group, count, 128), lambda g: (0, g, 0, 0))
+    return pl.pallas_call(
+        mix_kernel,
+        out_shape=jax.ShapeDtypeStruct(data.shape, BF16),
+        grid=(degrees // group,),
+        in_specs=[spec, pl.BlockSpec((group, 256, 256), lambda g: (g, 0, 0))],
+        out_specs=spec,
+        compiler_params=params(),
+        cost_estimate=cost(degrees * count * 4 * 256 * 256, degrees * 256 * 256 * 2),
+        name="mixing",
+    )(data, matrix)
+
+
+def synthesis_kernel(table, data, first, second, third):
+    for m in range(table.shape[0]):
+        value = lax.dot_general(
+            table[m], data[m], (((0,), (0,)), ((), ())), preferred_element_type=F32
+        ).astype(BF16)
+        depth = first.shape[1]
+        first[m] = value[:depth]
+        second[m] = value[depth : 2 * depth]
+        third[m] = value[2 * depth :]
+
+
+def synthesis_all(table, data, group=4):
+    count = table.shape[0]
+    depth = NLAT // PARTS
+    return pl.pallas_call(
+        synthesis_kernel,
+        out_shape=[jax.ShapeDtypeStruct((count, depth, 128), BF16)] * 3,
+        grid=(count // group,),
+        in_specs=[
+            pl.BlockSpec((group, L, NLAT), lambda g: (g, 0, 0)),
+            pl.BlockSpec((group, L, 128), lambda g: (g, 0, 0)),
+        ],
+        out_specs=[pl.BlockSpec((group, depth, 128), lambda g: (g, 0, 0))] * 3,
+        compiler_params=params(),
+        cost_estimate=cost(count * L * NLAT * 256, count * L * NLAT * 2),
+        name="synthesis",
+    )(table, data)
+
+
+def inverse_kernel(table, data, out):
+    columns = [[], []]
+    for r in range(2 * PAIRS):
+        row = jnp.concatenate([data[i, r] for i in range(8)], axis=0)
+        for p in range(2):
+            columns[p].append(row[:, 64 * p : 64 * p + 64])
+    joined = jnp.concatenate([jnp.concatenate(side, axis=1) for side in columns], axis=0)
+    for j in range(4):
+        value = jnp.dot(table[j], joined, preferred_element_type=F32).astype(BF16)
+        for g in range(PAIRS):
+            out[j, g] = value[:, 128 * g : 128 * g + 128]
+
+
+def inverse_part(table, data):
+    _, rows, orders, _ = data.shape
+    width = table.shape[1]
+    return pl.pallas_call(
+        inverse_kernel,
+        out_shape=jax.ShapeDtypeStruct((4, rows // 2, width, 128), BF16),
+        grid=(rows // (2 * PAIRS),),
+        in_specs=[
+            whole_block(table.shape),
+            pl.BlockSpec((8, 2 * PAIRS, orders, 128), lambda g: (0, g, 0, 0)),
+        ],
+        out_specs=pl.BlockSpec((4, PAIRS, width, 128), lambda g: (0, g, 0, 0)),
+        compiler_params=params(),
+        cost_estimate=cost(rows * 64 * 4 * width * 16 * orders * 2, rows * 64 * 4 * width * 4),
+        name="inverse_rows",
+    )(table, data)
+
+
+def join_kernel(data, prior, out):
+    for r in range(2):
+        out[r] = jnp.concatenate(
+            [data[j, 0][:, 64 * r : 64 * r + 64] for j in range(4)], axis=1
+        )
+
+
+def join_part(part, data, prior):
+    _, pairs, width, _ = data.shape
+    rows = 2 * pairs * PARTS
+    shape = jax.ShapeDtypeStruct((rows, width, 256), BF16)
+    first = prior is None
+    return pl.pallas_call(
+        (lambda data, out: join_kernel(data, None, out)) if first else join_kernel,
+        out_shape=shape,
+        grid=(pairs,),
+        in_specs=[pl.BlockSpec((4, 1, width, 128), lambda g: (0, g, 0, 0))]
+        + ([] if first else [pl.BlockSpec(memory_space=pl.ANY)]),
+        out_specs=pl.BlockSpec((2, width, 256), lambda g: (part * pairs + g, 0, 0)),
+        input_output_aliases={} if first else {1: 0},
+        compiler_params=params(),
+        cost_estimate=cost(0, pairs * width * 256 * 8),
+        name="join_rows",
+    )(*((data,) if first else (data, prior)))
+
+
+def swap(values, axis):
+    return lax.all_to_all(values, axis, split_axis=0, concat_axis=0, tiled=True)
+
+
+def fourier_pair(lon_count):
+    orders = jnp.arange(L, dtype=jnp.int32)
+    longitude = jnp.arange(NLON, dtype=jnp.int32).reshape(lon_count, 1, NLON // lon_count)
+    phase = (longitude * orders[None, :, None]) % NLON
+    angle = phase.astype(F32) * (2.0 * math.pi / NLON)
+    forward = jnp.concatenate([jnp.cos(angle), -jnp.sin(angle)], axis=1).astype(BF16)
+    factor = jnp.where(orders == 0, 1.0, 2.0).astype(BF16)
+    inverse = forward * jnp.tile(factor, 2)[None, :, None]
+    return forward, jnp.swapaxes(inverse, 1, 2)
+
+
+def packed_shards(cube_cells, block_source, block_weight, lift_in, lift_out, spectral):
+    lat_count = lax.axis_size("lat")
+    lon_count = lax.axis_size("lon")
+    lon_index = lax.axis_index("lon")
+    rows = block_weight.shape[0]
+    pairs = rows // (2 * PARTS)
+    per_band = L // lat_count
+    rim_tiles = SRC_DEV // 2
+    own_orders = lax.axis_index("lat") * per_band + jnp.arange(per_band, dtype=jnp.int32)
+
+    widened = extended(cube_cells, (("lon", 0),), rim_tiles)
+    picks = (block_source[:, 0, :] - lon_index * SRC_DEV + rim_tiles) % (lon_count * SRC_DEV)
+    picks = picks.reshape(-1)
+    weight = block_weight[:, 0]
+    forward, inverse = fourier_pair(lon_count)
+    row_order = jnp.arange(NLAT, dtype=jnp.int32).reshape(lat_count, PARTS, 2 * pairs)
+    row_order = jnp.swapaxes(row_order, 0, 1).reshape(NLAT)
+    table, quadrature = legendre_table(own_orders, row_order)
+    own_scale = lax.dynamic_slice_in_dim(quadrature, lax.axis_index("lat") * rows, rows)
+    own_scale = jnp.repeat(own_scale, 64).reshape(PARTS, pairs // PAIRS, 1, 128 * PAIRS)
+
+    pieces = []
+    for part in range(PARTS):
+        lifted = lift_part(part, pairs, picks, widened, weight, lift_in, lift_out)
+        spectra = dft_part(forward, swap(lifted, "lon"), own_scale[part])
+        gathered = swap(spectra, "lat").reshape(NLAT // PARTS, per_band, 128)
+        pieces.append(jnp.swapaxes(gathered, 0, 1))
+    analysis = analysis_all(table, pieces)
+    split = analysis.reshape(per_band, lon_count, L // lon_count, 128)
+    by_degree = swap(jnp.transpose(split, (1, 2, 0, 3)), "lon")
+    returned = swap(mix_all(by_degree, spectral), "lon").reshape(L, per_band, 128)
+    synthesized = synthesis_all(table, jnp.swapaxes(returned, 0, 1))
+    grid_field = None
+    for part in range(PARTS):
+        sent = jnp.swapaxes(synthesized[part], 0, 1)
+        sent = sent.reshape(lat_count, 2 * pairs, per_band, 128)
+        placed = inverse_part(inverse, swap(sent, "lat"))
+        grid_field = join_part(part, swap(placed, "lon"), grid_field)
+    return grid_field
+
+
 def solution(mesh):
+    packed = mesh.shape["lat"] == 8 and mesh.shape["lon"] == 4
     in_specs = (
         P(("lat", "lon"), None, None),
         P("lat", "lon", None),
@@ -233,4 +589,4 @@
         P("lon", None, None),
     )
     out_specs = P("lat", "lon", None)
-    return jax.shard_map(shards, mesh=mesh, in_specs=in_specs, out_specs=out_specs, check_vma=False)
+    return jax.shard_map(packed_shards if packed else shards, mesh=mesh, in_specs=in_specs, out_specs=out_specs, check_vma=False)

time: 2120 us -> 1070 us (0.50)
  local copies, waits for them, and re-layouts: 587 us -> 57 us
  blocking collectives: 405 us -> 115 us
  loops' own time: 258 us -> 0 us
  Pallas kernels: 0 us -> 251 us
  matrix products: 188 us -> 0 us
  other arithmetic: 197 us -> 15.4 us
  waiting for transfers between devices: 442 us -> 569 us
  starting transfers between devices: 21.2 us -> 59.5 us
    all_to_all x3 -> x2, blocking collectives: 405 us -> 115 us  [swap(): return lax.all_to_all(values, axis, split_axis=0, concat_axis=0, tiled=True)]
    another operation x5 -> x0, loops' own time: 258 us -> none  [the longest x1 257 us: legendre_tables(): lax.scan(advance, (zeroed, zeroed), jnp.arange(0, L, unroll_steps, dtype=...]
    pallas_call x0 -> x16, Pallas kernels: none -> 251 us  [the longest x3 63.9 us: lift_part(): pl.pallas_call(lambda *refs: lift_kernel(part * pairs * 2, *refs), out_sh...]
    all_to_all x11 -> x1, local copies, waits for them, and re-layouts: 213 us -> 3.4 us  [swap(): return lax.all_to_all(values, axis, split_axis=0, concat_axis=0, tiled=True)]
    dot_general x17 -> x0, matrix products: 188 us -> none  [the longest x6 62.8 us: add_block(): jnp.einsum('lmt,mlpd->mpdt', table_block, degree_rows, preferred_element_...]
    all_to_all x3 -> x12, waiting for transfers between devices: 432 us -> 559 us  [swap(): return lax.all_to_all(values, axis, split_axis=0, concat_axis=0, tiled=True)]
    convert_element_type x6 -> x0, local copies, waits for them, and re-layouts: 101 us -> none  [the longest x1 30.9 us: shards(): grid_field = jnp.einsum('qcr,kq->rkc', rows_back, inverse, preferred_elem...]
    slice x9 -> x2, local copies, waits for them, and re-layouts: 69.1 us -> 1.4 us  [the longest x1 1.33 us: extended(): head = lax.slice_in_dim(cells, 0, width, axis=dim)]
  transfers between devices with their start and end apart: 5 -> 14, of which waited for: 4 -> 14; matrix products, arithmetic and copies ran while one was open for 14% -> 5% of each run, Pallas kernels for 0% -> 16%
where the time goes in v1:
time: 1070 us
  waiting for transfers between devices  569 us (53%)
  Pallas kernels  251 us (23%)
  blocking collectives  115 us (11%)
  starting transfers between devices  59.5 us (6%)
  local copies, waits for them, and re-layouts  57 us (5%)
  other arithmetic  15.4 us (1%)
    all_to_all x12, waiting for transfers between devices, swap(): return lax.all_to_all(values, axis, split_axis=0, concat_axis=0, tiled=True)  559 us
    all_to_all x2, blocking collectives, swap(): return lax.all_to_all(values, axis, split_axis=0, concat_axis=0, tiled=True)  115 us
    pallas_call x3, Pallas kernels, lift_part(): pl.pallas_call(lambda *refs: lift_kernel(part * pairs * 2, *refs), out_sh...  63.9 us
    all_to_all x12, starting transfers between devices, swap(): return lax.all_to_all(values, axis, split_axis=0, concat_axis=0, tiled=True)  57 us
    pallas_call x1, Pallas kernels, legendre_table(): pl.pallas_call(legendre_kernel, out_shape=jax.ShapeDtypeStruct((count, L,...  36.6 us
    pallas_call x3, Pallas kernels, dft_part(): pl.pallas_call(dft_kernel, out_shape=jax.ShapeDtypeStruct((8, 2 * pairs,...  34.1 us
    pallas_call x3, Pallas kernels, join_part(): pl.pallas_call((lambda data, out: join_kernel(data, None, out)) if first...  33.9 us
    pallas_call x3, Pallas kernels, inverse_part(): pl.pallas_call(inverse_kernel, out_shape=jax.ShapeDtypeStruct((4, rows //...  30.3 us
  transfers between devices with their start and end apart: 14, of which 14 were waited for; matrix products, arithmetic and copies ran while one was open for 5% of the time, Pallas kernels for 16%

profile of v1, /device:TPU:0, one launch (start us, length us, event | category | flops | bytes accessed | tf_op | source)
XLA Modules:
  0.0 1066.5 jit_solution(18351722135030887530)
XLA Ops:
  0.0 1.3 fusion.15
  1.8 2.0 collective-permute-start.1
  5.3 7.5 collective-permute-done
  13.1 2.3 collective-permute-done.1
  15.4 1.3 copy-done
  16.7 21.3 %lift_rows.5 = bf16[4,15,360,128]{3,2,1,0:T(8,128)(2,1)} custom-call(s32[360]{0:T(512)} %add_select_fusion.1.refs_0_, bf16[96,80,128]{2,1,0:T(8,128)(2,1)} %copy-done, bf16[90,4,360,128]{3,2,1,0:T(8,128)(2,1)} %bitcast.31, bf16[80,256]{1,0:T(8,128)(2,1)} %refs_3_.5, bf16[256,256]{1,0:T(8,128)(2,1)} %refs_4_.5), custom_call_target="tpu_custom_call" | custom-call | flops 2831155200 | bytes 16588800 | tf_op jit(solution)/shard_map/lift_rows/pallas_call | solution.py:271
  38.0 5.1 all-to-all-start.4
  43.1 21.3 %lift_rows.4 = bf16[4,15,360,128]{3,2,1,0:T(8,128)(2,1)} custom-call(s32[360]{0:T(512)} %add_select_fusion.1.refs_0_, bf16[96,80,128]{2,1,0:T(8,128)(2,1)} %copy-done, bf16[90,4,360,128]{3,2,1,0:T(8,128)(2,1)} %bitcast.32, bf16[80,256]{1,0:T(8,128)(2,1)} %refs_3_.5, bf16[256,256]{1,0:T(8,128)(2,1)} %refs_4_.5), custom_call_target="tpu_custom_call" | custom-call | flops 2831155200 | bytes 16588800 | tf_op jit(solution)/shard_map/lift_rows/pallas_call | solution.py:271
  64.5 41.5 %all-to-all-done.4.data = bf16[4,15,360,128]{3,2,1,0:T(8,128)(2,1)} async-done(((bf16[4,15,360,128]{3,2,1,0:T(8,128)(2,1)}), bf16[4,15,360,128]{3,2,1,0:T(8,128)(2,1)}, u32[]{:S(2)}, u32[]{:S(2)}) %all-to-all-start.4) | async-done | bytes 5529632 | tf_op jit(solution)/shard_map/all_to_all | solution.py:526
  106.0 5.1 all-to-all-start.2
  111.1 21.3 %lift_rows.3 = bf16[4,15,360,128]{3,2,1,0:T(8,128)(2,1)} custom-call(s32[360]{0:T(512)} %add_select_fusion.1.refs_0_, bf16[96,80,128]{2,1,0:T(8,128)(2,1)} %copy-done, bf16[90,4,360,128]{3,2,1,0:T(8,128)(2,1)} %bitcast.33, bf16[80,256]{1,0:T(8,128)(2,1)} %refs_3_.5, bf16[256,256]{1,0:T(8,128)(2,1)} %refs_4_.5), custom_call_target="tpu_custom_call" | custom-call | flops 2831155200 | bytes 16588800 | tf_op jit(solution)/shard_map/lift_rows/pallas_call | solution.py:271
  132.5 41.2 %all-to-all-done.2.data = bf16[4,15,360,128]{3,2,1,0:T(8,128)(2,1)} async-done(((bf16[4,15,360,128]{3,2,1,0:T(8,128)(2,1)}), bf16[4,15,360,128]{3,2,1,0:T(8,128)(2,1)}, u32[]{:S(2)}, u32[]{:S(2)}) %all-to-all-start.2) | async-done | bytes 5529632 | tf_op jit(solution)/shard_map/all_to_all | solution.py:526
  173.7 5.1 all-to-all-start
  179.9 10.4 cosine_convert_fusion
  190.3 2.0 pad_maximum_fusion
  192.3 2.5 copy.41.table
  194.8 11.4 %forward_rows.5 = bf16[8,30,48,128]{3,2,1,0:T(8,128)(2,1)} custom-call(bf16[4,768,360]{2,1,0:T(8,128)(2,1)} %copy.41.table, bf16[4,15,360,128]{3,2,1,0:T(8,128)(2,1)} %all-to-all-done.4.data, f32[5,1,384]{2,1,0:T(1,128)} %broadcast_in_dim.44.scale), custom_call_target="tpu_custom_call" | custom-call | flops 4246732800 | bytes 11059200 | tf_op jit(solution)/shard_map/forward_rows/pallas_call | solution.py:310
  206.2 35.2 %all-to-all-done.data = bf16[4,15,360,128]{3,2,1,0:T(8,128)(2,1)} async-done(((bf16[4,15,360,128]{3,2,1,0:T(8,128)(2,1)}), bf16[4,15,360,128]{3,2,1,0:T(8,128)(2,1)}, u32[]{:S(2)}, u32[]{:S(2)}) %all-to-all-start) | async-done | bytes 5529632 | tf_op jit(solution)/shard_map/all_to_all | solution.py:526
  241.4 5.6 all-to-all-start.5
  247.8 11.4 %forward_rows.4 = bf16[8,30,48,128]{3,2,1,0:T(8,128)(2,1)} custom-call(bf16[4,768,360]{2,1,0:T(8,128)(2,1)} %copy.41.table, bf16[4,15,360,128]{3,2,1,0:T(8,128)(2,1)} %all-to-all-done.2.data, f32[5,1,384]{2,1,0:T(1,128)} %broadcast_in_dim.41.scale), custom_call_target="tpu_custom_call" | custom-call | flops 4246732800 | bytes 11059200 | tf_op jit(solution)/shard_map/forward_rows/pallas_call | solution.py:310
  259.2 54.1 %all-to-all-done.5 = bf16[8,30,48,128]{3,2,1,0:T(8,128)(2,1)S(1)} async-done(((bf16[8,30,48,128]{3,2,1,0:T(8,128)(2,1)}), bf16[8,30,48,128]{3,2,1,0:T(8,128)(2,1)S(1)}, u32[]{:S(2)}, u32[]{:S(2)}) %all-to-all-start.5) | async-done | bytes 2949152 | tf_op jit(solution)/shard_map/all_to_all | solution.py:526
  313.3 4.4 all-to-all-start.3
  318.5 11.4 %forward_rows.3 = bf16[8,30,48,128]{3,2,1,0:T(8,128)(2,1)} custom-call(bf16[4,768,360]{2,1,0:T(8,128)(2,1)} %copy.41.table, bf16[4,15,360,128]{3,2,1,0:T(8,128)(2,1)} %all-to-all-done.data, f32[5,1,384]{2,1,0:T(1,128)} %broadcast_in_dim.38.scale), custom_call_target="tpu_custom_call" | custom-call | flops 4246732800 | bytes 11059200 | tf_op jit(solution)/shard_map/forward_rows/pallas_call | solution.py:310
  329.9 53.8 %all-to-all-done.3 = bf16[8,30,48,128]{3,2,1,0:T(8,128)(2,1)} async-done(((bf16[8,30,48,128]{3,2,1,0:T(8,128)(2,1)}), bf16[8,30,48,128]{3,2,1,0:T(8,128)(2,1)}, u32[]{:S(2)}, u32[]{:S(2)}) %all-to-all-start.3) | async-done | bytes 2949152 | tf_op jit(solution)/shard_map/all_to_all | solution.py:526
  383.7 4.6 all-to-all-start.1
  388.6 3.2 gather_fusion
  393.8 2.3 gather_fusion.2
  396.1 1.1 copy.39
  398.6 2.3 gather_fusion.1
  403.3 36.6 %legendre_table.1.table = bf16[48,384,720]{2,1,0:T(8,128)(2,1)} custom-call(f32[1,768]{1,0:T(1,128)} %pad.11.cosine, f32[48,1]{1,0:T(8,128)} %add_convert_fusion.order, f32[48,768]{1,0:T(8,128)} %pad.12.initial, f32[48,768]{1,0:T(8,128)} %pad.13.restore), custom_call_target="tpu_custom_call" | custom-call | flops 1415577600 | bytes 26542080 | tf_op jit(solution)/shard_map/legendre_table/pallas_call | solution.py:365
  439.9 2.3 copy.55
  442.3 4.3 copy.56
  446.5 7.7 all-to-all-done.1
  454.2 4.3 copy.57
  458.5 19.0 %analysis.1 = bf16[48,384,128]{2,1,0:T(8,128)(2,1)} custom-call(bf16[48,384,720]{2,1,0:T(8,128)(2,1)} %legendre_table.1.table, bf16[48,240,128]{2,1,0:T(8,128)(2,1)} %bitcast.39, bf16[48,240,128]{2,1,0:T(8,128)(2,1)} %bitcast.38, bf16[48,240,128]{2,1,0:T(8,128)(2,1)} %bitcast.37), custom_call_target="tpu_custom_call" | custom-call | flops 3397386240 | bytes 26542080 | tf_op jit(solution)/shard_map/analysis/pallas_call | solution.py:397
  477.5 5.4 copy.47
  482.8 57.3 %all_to_all.70.data = bf16[4,96,48,128]{3,2,1,0:T(8,128)(2,1)} all-to-all(bf16[4,96,48,128]{3,2,1,0:T(8,128)(2,1)S(1)} %bitcast.34), channel_id=1, replica_groups=mesh['lat'=8,'lon'=4] {'lon'}, dimensions={0} | all-to-all | bytes 9437184 | tf_op jit(solution)/shard_map/all_to_all | solution.py:526
  540.1 13.3 %mixing.1 = bf16[4,96,48,128]{3,2,1,0:T(8,128)(2,1)} custom-call(bf16[4,96,48,128]{3,2,1,0:T(8,128)(2,1)} %all_to_all.70.data, bf16[96,256,256]{2,1,0:T(8,128)(2,1)} %matrix.1), custom_call_target="tpu_custom_call" | custom-call | flops 1207959552 | bytes 12582912 | tf_op jit(solution)/shard_map/mixing/pallas_call | solution.py:427
  553.4 57.6 %all_to_all.71 = bf16[4,96,48,128]{3,2,1,0:T(8,128)(2,1)S(1)} all-to-all(bf16[4,96,48,128]{3,2,1,0:T(8,128)(2,1)} %mixing.1), channel_id=1, replica_groups=mesh['lat'=8,'lon'=4] {'lon'}, dimensions={0} | all-to-all | bytes 9437184 | tf_op jit(solution)/shard_map/all_to_all | solution.py:526
  611.0 3.4 copy.48
  614.4 19.6 %synthesis.1 = (bf16[48,240,128]{2,1,0:T(8,128)(2,1)}, bf16[48,240,128]{2,1,0:T(8,128)(2,1)}, bf16[48,240,128]{2,1,0:T(8,128)(2,1)}) custom-call(bf16[48,384,720]{2,1,0:T(8,128)(2,1)} %legendre_table.1.table, bf16[48,384,128]{2,1,0:T(8,128)(2,1)} %bitcast.35), custom_call_target="tpu_custom_call" | custom-call | flops 3397386240 | bytes 26542080 | tf_op jit(solution)/shard_map/synthesis/pallas_call | solution.py:453
  634.0 4.2 copy.50
  638.2 3.6 all-to-all-start.10
  641.9 4.2 copy.49
  646.0 62.1 %all-to-all-done.10.data = bf16[8,30,48,128]{3,2,1,0:T(8,128)(2,1)S(1)} async-done(((bf16[8,30,48,128]{3,2,1,0:T(8,128)(2,1)}), bf16[8,30,48,128]{3,2,1,0:T(8,128)(2,1)S(1)}, u32[]{:S(2)}, u32[]{:S(2)}) %all-to-all-start.10) | async-done | bytes 2949152 | tf_op jit(solution)/shard_map/all_to_all | solution.py:526
  708.2 1.7 copy-done.3
  709.8 3.6 all-to-all-start.8
  713.5 4.2 copy.51
  717.7 62.5 %all-to-all-done.8.data = bf16[8,30,48,128]{3,2,1,0:T(8,128)(2,1)S(1)} async-done(((bf16[8,30,48,128]{3,2,1,0:T(8,128)(2,1)}), bf16[8,30,48,128]{3,2,1,0:T(8,128)(2,1)S(1)}, u32[]{:S(2)}, u32[]{:S(2)}) %all-to-all-start.8) | async-done | bytes 2949152 | tf_op jit(solution)/shard_map/all_to_all | solution.py:526
  780.1 1.6 copy-done.2
  781.8 4.4 all-to-all-start.12
  786.2 10.1 inverse_rows.4
  796.3 55.9 %all-to-all-done.12.data = bf16[8,30,48,128]{3,2,1,0:T(8,128)(2,1)} async-done(((bf16[8,30,48,128]{3,2,1,0:T(8,128)(2,1)}), bf16[8,30,48,128]{3,2,1,0:T(8,128)(2,1)}, u32[]{:S(2)}, u32[]{:S(2)}) %all-to-all-start.12) | async-done | bytes 2949152 | tf_op jit(solution)/shard_map/all_to_all | solution.py:526
  852.2 5.1 all-to-all-start.11
  857.3 10.1 inverse_rows.5
  867.5 52.4 %all-to-all-done.11.data = bf16[4,15,360,128]{3,2,1,0:T(8,128)(2,1)} async-done(((bf16[4,15,360,128]{3,2,1,0:T(8,128)(2,1)}), bf16[4,15,360,128]{3,2,1,0:T(8,128)(2,1)}, u32[]{:S(2)}, u32[]{:S(2)}) %all-to-all-start.11) | async-done | bytes 5529632 | tf_op jit(solution)/shard_map/all_to_all | solution.py:526
  919.9 5.1 all-to-all-start.13
  925.0 10.1 inverse_rows.3
  935.1 52.4 %all-to-all-done.13.data = bf16[4,15,360,128]{3,2,1,0:T(8,128)(2,1)} async-done(((bf16[4,15,360,128]{3,2,1,0:T(8,128)(2,1)}), bf16[4,15,360,128]{3,2,1,0:T(8,128)(2,1)}, u32[]{:S(2)}, u32[]{:S(2)}) %all-to-all-start.13) | async-done | bytes 5529632 | tf_op jit(solution)/shard_map/all_to_all | solution.py:526
  987.5 5.1 all-to-all-start.9
  992.6 11.3 %join_rows.3.prior = bf16[90,360,256]{2,1,0:T(8,128)(2,1)} custom-call(bf16[4,15,360,128]{3,2,1,0:T(8,128)(2,1)} %all-to-all-done.13.data), custom_call_target="tpu_custom_call" | custom-call | bytes 11059200 | tf_op jit(solution)/shard_map/join_rows/pallas_call | solution.py:511
  1003.9 11.3 %join_rows.4.prior = bf16[90,360,256]{2,1,0:T(8,128)(2,1)} custom-call(bf16[4,15,360,128]{3,2,1,0:T(8,128)(2,1)} %all-to-all-done.11.data, bf16[90,360,256]{2,1,0:T(8,128)(2,1)} %join_rows.3.prior), custom_call_target="tpu_custom_call", output_to_operand_aliasing={{}: (1, {})} | custom-call | bytes 11059200 | tf_op jit(solution)/shard_map/join_rows/pallas_call | solution.py:511
  1015.2 39.9 %all-to-all-done.9.data = bf16[4,15,360,128]{3,2,1,0:T(8,128)(2,1)} async-done(((bf16[4,15,360,128]{3,2,1,0:T(8,128)(2,1)}), bf16[4,15,360,128]{3,2,1,0:T(8,128)(2,1)}, u32[]{:S(2)}, u32[]{:S(2)}) %all-to-all-start.9) | async-done | bytes 5529632 | tf_op jit(solution)/shard_map/all_to_all | solution.py:526
  1055.2 11.3 %join_rows.5 = bf16[90,360,256]{2,1,0:T(8,128)(2,1)} custom-call(bf16[4,15,360,128]{3,2,1,0:T(8,128)(2,1)} %all-to-all-done.9.data, bf16[90,360,256]{2,1,0:T(8,128)(2,1)} %join_rows.4.prior), custom_call_target="tpu_custom_call", output_to_operand_aliasing={{}: (1, {})} | custom-call | bytes 11059200 | tf_op jit(solution)/shard_map/join_rows/pallas_call | solution.py:511
  (46 shorter events, 11.0 us)
Async XLA Ops:
  0.0 12.9 %copy-start.1 = (bf16[48,80,128]{2,1,0:T(8,128)(2,1)S(1)}, bf16[48,80,128]{2,1,0:T(8,128)(2,1)}, u32[]{:S(2)}) copy-start(bf16[48,80,128]{2,1,0:T(8,128)(2,1)} %param.6) | copy-start | bytes 2949124
  1.3 11.5 %collective-permute-start = (bf16[24,80,128]{2,1,0:T(8,128)(2,1)S(1)}, bf16[24,80,128]{2,1,0:T(8,128)(2,1)S(1)}, u32[]{:S(2)}, u32[]{:S(2)}) collective-permute-start(bf16[24,80,128]{2,1,0:T(8,128)(2,1)S(1)} %get-tuple-element.14), channel_id=1, source_target_pairs={{0,1},{1,2},{2,3},{3,0},{4,5},{5,6},{6,7},{7,4},{8,9},{9,10},{10,1... | collective-permute-start | bytes 1474568 | tf_op jit(solution)/shard_map/ppermute | solution.py:26
  1.8 13.5 %collective-permute-start.1 = (bf16[24,80,128]{2,1,0:T(8,128)(2,1)S(1)}, bf16[24,80,128]{2,1,0:T(8,128)(2,1)S(1)}, u32[]{:S(2)}, u32[]{:S(2)}) collective-permute-start(bf16[24,80,128]{2,1,0:T(8,128)(2,1)S(1)} %get-tuple-element.13), channel_id=1, source_target_pairs={{1,0},{2,1},{3,2},{0,3},{5,4},{6,5},{7,6},{4,7},{9,8},{10,9},{11,1... | collective-permute-start | bytes 1474568 | tf_op jit(solution)/shard_map/ppermute | solution.py:28
  15.4 1.3 copy-start
  38.0 68.0 %all-to-all-start.4 = ((bf16[4,15,360,128]{3,2,1,0:T(8,128)(2,1)}), bf16[4,15,360,128]{3,2,1,0:T(8,128)(2,1)}, u32[]{:S(2)}, u32[]{:S(2)}) async-start(bf16[4,15,360,128]{3,2,1,0:T(8,128)(2,1)} %lift_rows.5), calls=%async_computation.4 | async-start | bytes 11059200 | tf_op jit(solution)/shard_map/all_to_all | solution.py:526
  106.0 67.7 %all-to-all-start.2 = ((bf16[4,15,360,128]{3,2,1,0:T(8,128)(2,1)}), bf16[4,15,360,128]{3,2,1,0:T(8,128)(2,1)}, u32[]{:S(2)}, u32[]{:S(2)}) async-start(bf16[4,15,360,128]{3,2,1,0:T(8,128)(2,1)} %lift_rows.4), calls=%async_computation.2 | async-start | bytes 11059200 | tf_op jit(solution)/shard_map/all_to_all | solution.py:526
  173.7 67.7 %all-to-all-start = ((bf16[4,15,360,128]{3,2,1,0:T(8,128)(2,1)}), bf16[4,15,360,128]{3,2,1,0:T(8,128)(2,1)}, u32[]{:S(2)}, u32[]{:S(2)}) async-start(bf16[4,15,360,128]{3,2,1,0:T(8,128)(2,1)} %lift_rows.3), calls=%async_computation | async-start | bytes 11059200 | tf_op jit(solution)/shard_map/all_to_all | solution.py:526
  241.4 71.9 %all-to-all-start.5 = ((bf16[8,30,48,128]{3,2,1,0:T(8,128)(2,1)}), bf16[8,30,48,128]{3,2,1,0:T(8,128)(2,1)S(1)}, u32[]{:S(2)}, u32[]{:S(2)}) async-start(bf16[8,30,48,128]{3,2,1,0:T(8,128)(2,1)} %forward_rows.5), calls=%async_computation.5 | async-start | bytes 5898240 | tf_op jit(solution)/shard_map/all_to_all | solution.py:526
  313.3 70.4 %all-to-all-start.3 = ((bf16[8,30,48,128]{3,2,1,0:T(8,128)(2,1)}), bf16[8,30,48,128]{3,2,1,0:T(8,128)(2,1)}, u32[]{:S(2)}, u32[]{:S(2)}) async-start(bf16[8,30,48,128]{3,2,1,0:T(8,128)(2,1)} %forward_rows.4), calls=%async_computation.3 | async-start | bytes 5898240 | tf_op jit(solution)/shard_map/all_to_all | solution.py:526
  383.7 70.5 %all-to-all-start.1 = ((bf16[8,30,48,128]{3,2,1,0:T(8,128)(2,1)}), bf16[8,30,48,128]{3,2,1,0:T(8,128)(2,1)}, u32[]{:S(2)}, u32[]{:S(2)}) async-start(bf16[8,30,48,128]{3,2,1,0:T(8,128)(2,1)} %forward_rows.3), calls=%async_computation.1 | async-start | bytes 5898240 | tf_op jit(solution)/shard_map/all_to_all | solution.py:526
  638.2 70.0 %all-to-all-start.10 = ((bf16[8,30,48,128]{3,2,1,0:T(8,128)(2,1)}), bf16[8,30,48,128]{3,2,1,0:T(8,128)(2,1)S(1)}, u32[]{:S(2)}, u32[]{:S(2)}) async-start(bf16[8,30,48,128]{3,2,1,0:T(8,128)(2,1)} %bitcast.17), calls=%async_computation.10 | async-start | bytes 5898240 | tf_op jit(solution)/shard_map/all_to_all | solution.py:526
  708.2 1.7 copy-start.3
  709.8 70.3 %all-to-all-start.8 = ((bf16[8,30,48,128]{3,2,1,0:T(8,128)(2,1)}), bf16[8,30,48,128]{3,2,1,0:T(8,128)(2,1)S(1)}, u32[]{:S(2)}, u32[]{:S(2)}) async-start(bf16[8,30,48,128]{3,2,1,0:T(8,128)(2,1)} %bitcast.15), calls=%async_computation.8 | async-start | bytes 5898240 | tf_op jit(solution)/shard_map/all_to_all | solution.py:526
  780.1 1.7 copy-start.2
  781.8 70.4 %all-to-all-start.12 = ((bf16[8,30,48,128]{3,2,1,0:T(8,128)(2,1)}), bf16[8,30,48,128]{3,2,1,0:T(8,128)(2,1)}, u32[]{:S(2)}, u32[]{:S(2)}) async-start(bf16[8,30,48,128]{3,2,1,0:T(8,128)(2,1)} %bitcast.19), calls=%async_computation.12 | async-start | bytes 5898240 | tf_op jit(solution)/shard_map/all_to_all | solution.py:526
  852.2 67.7 %all-to-all-start.11 = ((bf16[4,15,360,128]{3,2,1,0:T(8,128)(2,1)}), bf16[4,15,360,128]{3,2,1,0:T(8,128)(2,1)}, u32[]{:S(2)}, u32[]{:S(2)}) async-start(bf16[4,15,360,128]{3,2,1,0:T(8,128)(2,1)} %inverse_rows.4), calls=%async_computation.11 | async-start | bytes 11059200 | tf_op jit(solution)/shard_map/all_to_all | solution.py:526
  919.9 67.6 %all-to-all-start.13 = ((bf16[4,15,360,128]{3,2,1,0:T(8,128)(2,1)}), bf16[4,15,360,128]{3,2,1,0:T(8,128)(2,1)}, u32[]{:S(2)}, u32[]{:S(2)}) async-start(bf16[4,15,360,128]{3,2,1,0:T(8,128)(2,1)} %inverse_rows.5), calls=%async_computation.13 | async-start | bytes 11059200 | tf_op jit(solution)/shard_map/all_to_all | solution.py:526
  987.5 67.6 %all-to-all-start.9 = ((bf16[4,15,360,128]{3,2,1,0:T(8,128)(2,1)}), bf16[4,15,360,128]{3,2,1,0:T(8,128)(2,1)}, u32[]{:S(2)}, u32[]{:S(2)}) async-start(bf16[4,15,360,128]{3,2,1,0:T(8,128)(2,1)} %inverse_rows.3), calls=%async_computation.9 | async-start | bytes 11059200 | tf_op jit(solution)/shard_map/all_to_all | solution.py:526

commit v2 on v1

--- a/solution.py
+++ b/solution.py
@@ -249,7 +249,7 @@
     return jnp.concatenate([left[:, at : at + 64], right[:, at : at + 64]], axis=1)
 
 
-def lift_kernel(first_row, picks, tiles, weight, lift_in, lift_out, out):
+def lift_kernel(first_row, picks, tiles, weight, lift_in, lift_out, *outs):
     rows = []
     for r in range(2):
         row = first_row + pl.program_id(0) * 2 + r
@@ -263,14 +263,14 @@
             jnp.dot(hidden.astype(BF16), lift_out[...], preferred_element_type=F32).astype(BF16)
         )
     for q in range(4):
-        out[q, 0] = halves(rows[0], rows[1], 64 * q)
+        outs[q][0] = halves(rows[0], rows[1], 64 * q)
 
 
 def lift_part(part, pairs, picks, tiles, weight, lift_in, lift_out):
     width = weight.shape[2]
     return pl.pallas_call(
         lambda *refs: lift_kernel(part * pairs * 2, *refs),
-        out_shape=jax.ShapeDtypeStruct((4, pairs, width, 128), BF16),
+        out_shape=[jax.ShapeDtypeStruct((pairs, width, 128), BF16)] * 4,
         grid_spec=pltpu.PrefetchScalarGridSpec(
             num_scalar_prefetch=1,
             grid=(pairs,),
@@ -280,7 +280,7 @@
                 whole_block(lift_in.shape),
                 whole_block(lift_out.shape),
             ],
-            out_specs=pl.BlockSpec((4, 1, width, 128), lambda g, _: (0, g, 0, 0)),
+            out_specs=[pl.BlockSpec((1, width, 128), lambda g, _: (g, 0, 0))] * 4,
         ),
         compiler_params=params(),
         cost_estimate=cost(pairs * 2 * width * 256 * 256 * 4, pairs * width * 128 * 24),
@@ -288,10 +288,11 @@
     )(picks, tiles, weight, lift_in, lift_out)
 
 
-def dft_kernel(table, data, scale, out):
+def dft_kernel(table, scale, first, second, third, fourth, out):
+    data = (first, second, third, fourth)
     total = None
     for j in range(4):
-        block = jnp.concatenate([data[j, g] for g in range(PAIRS)], axis=1)
+        block = jnp.concatenate([data[j][g] for g in range(PAIRS)], axis=1)
         term = jnp.dot(table[j], block, preferred_element_type=F32)
         total = term if total is None else total + term
     total = total * scale[0]
@@ -304,7 +305,7 @@
 
 
 def dft_part(table, data, scale):
-    _, pairs, width, _ = data.shape
+    pairs, width, _ = data[0].shape
     waves = table.shape[1]
     rows = 2 * PAIRS
     return pl.pallas_call(
@@ -313,14 +314,14 @@
         grid=(pairs // PAIRS,),
         in_specs=[
             whole_block(table.shape),
-            pl.BlockSpec((4, PAIRS, width, 128), lambda g: (0, g, 0, 0)),
             pl.BlockSpec((1, 1, 64 * rows), lambda g: (g, 0, 0)),
-        ],
+        ]
+        + [pl.BlockSpec((PAIRS, width, 128), lambda g: (g, 0, 0))] * 4,
         out_specs=pl.BlockSpec((8, rows, waves // 16, 128), lambda g: (0, g, 0, 0)),
         compiler_params=params(),
         cost_estimate=cost(pairs * 128 * 4 * width * waves * 2, pairs * 128 * 4 * width * 4),
         name="forward_rows",
-    )(table, data, scale)
+    )(table, scale, *data)
 
 
 def legendre_kernel(cosine, order, initial, restore, out, current, earlier, held):
@@ -465,7 +466,7 @@
     )(table, data)
 
 
-def inverse_kernel(table, data, out):
+def inverse_kernel(table, data, *outs):
     columns = [[], []]
     for r in range(2 * PAIRS):
         row = jnp.concatenate([data[i, r] for i in range(8)], axis=0)
@@ -475,7 +476,7 @@
     for j in range(4):
         value = jnp.dot(table[j], joined, preferred_element_type=F32).astype(BF16)
         for g in range(PAIRS):
-            out[j, g] = value[:, 128 * g : 128 * g + 128]
+            outs[j][g] = value[:, 128 * g : 128 * g + 128]
 
 
 def inverse_part(table, data):
@@ -483,52 +484,68 @@
     width = table.shape[1]
     return pl.pallas_call(
         inverse_kernel,
-        out_shape=jax.ShapeDtypeStruct((4, rows // 2, width, 128), BF16),
+        out_shape=[jax.ShapeDtypeStruct((rows // 2, width, 128), BF16)] * 4,
         grid=(rows // (2 * PAIRS),),
         in_specs=[
             whole_block(table.shape),
             pl.BlockSpec((8, 2 * PAIRS, orders, 128), lambda g: (0, g, 0, 0)),
         ],
-        out_specs=pl.BlockSpec((4, PAIRS, width, 128), lambda g: (0, g, 0, 0)),
+        out_specs=[pl.BlockSpec((PAIRS, width, 128), lambda g: (g, 0, 0))] * 4,
         compiler_params=params(),
         cost_estimate=cost(rows * 64 * 4 * width * 16 * orders * 2, rows * 64 * 4 * width * 4),
         name="inverse_rows",
     )(table, data)
 
 
-def join_kernel(data, prior, out):
-    for r in range(2):
-        out[r] = jnp.concatenate(
-            [data[j, 0][:, 64 * r : 64 * r + 64] for j in range(4)], axis=1
-        )
-
-
-def join_part(part, data, prior):
-    _, pairs, width, _ = data.shape
-    rows = 2 * pairs * PARTS
-    shape = jax.ShapeDtypeStruct((rows, width, 256), BF16)
+def join_kernel(place, *refs):
+    data, out = refs[:4], refs[-1]
+    for here in range(4):
+
+        @pl.when(place[0] == here)
+        def _():
+            blocks = [data[here ^ j][0] for j in range(4)]
+            for r in range(2):
+                out[r] = jnp.concatenate(
+                    [block[:, 64 * r : 64 * r + 64] for block in blocks], axis=1
+                )
+
+
+def join_part(part, place, data, prior):
+    pairs, width, _ = data[0].shape
     first = prior is None
     return pl.pallas_call(
-        (lambda data, out: join_kernel(data, None, out)) if first else join_kernel,
-        out_shape=shape,
-        grid=(pairs,),
-        in_specs=[pl.BlockSpec((4, 1, width, 128), lambda g: (0, g, 0, 0))]
-        + ([] if first else [pl.BlockSpec(memory_space=pl.ANY)]),
-        out_specs=pl.BlockSpec((2, width, 256), lambda g: (part * pairs + g, 0, 0)),
-        input_output_aliases={} if first else {1: 0},
+        join_kernel,
+        out_shape=jax.ShapeDtypeStruct((2 * pairs * PARTS, width, 256), BF16),
+        grid_spec=pltpu.PrefetchScalarGridSpec(
+            num_scalar_prefetch=1,
+            grid=(pairs,),
+            in_specs=[pl.BlockSpec((1, width, 128), lambda g, _: (g, 0, 0))] * 4
+            + ([] if first else [pl.BlockSpec(memory_space=pl.ANY)]),
+            out_specs=pl.BlockSpec((2, width, 256), lambda g, _: (part * pairs + g, 0, 0)),
+        ),
+        input_output_aliases={} if first else {5: 0},
         compiler_params=params(),
         cost_estimate=cost(0, pairs * width * 256 * 8),
         name="join_rows",
-    )(*((data,) if first else (data, prior)))
+    )(place, *data, *(() if first else (prior,)))
+
+
+def exchange(pieces, axis):
+    count = lax.axis_size(axis)
+    return [pieces[0]] + [
+        lax.ppermute(pieces[s], axis, [(i, i ^ s) for i in range(count)])
+        for s in range(1, count)
+    ]
 
 
 def swap(values, axis):
     return lax.all_to_all(values, axis, split_axis=0, concat_axis=0, tiled=True)
 
 
-def fourier_pair(lon_count):
+def fourier_pair(blocks):
     orders = jnp.arange(L, dtype=jnp.int32)
-    longitude = jnp.arange(NLON, dtype=jnp.int32).reshape(lon_count, 1, NLON // lon_count)
+    width = NLON // blocks.shape[0]
+    longitude = blocks[:, None, None] * width + jnp.arange(width, dtype=jnp.int32)
     phase = (longitude * orders[None, :, None]) % NLON
     angle = phase.astype(F32) * (2.0 * math.pi / NLON)
     forward = jnp.concatenate([jnp.cos(angle), -jnp.sin(angle)], axis=1).astype(BF16)
@@ -551,7 +568,10 @@
     picks = (block_source[:, 0, :] - lon_index * SRC_DEV + rim_tiles) % (lon_count * SRC_DEV)
     picks = picks.reshape(-1)
     weight = block_weight[:, 0]
-    forward, inverse = fourier_pair(lon_count)
+    blocks = lon_index ^ jnp.arange(lon_count, dtype=jnp.int32)
+    forward, inverse = fourier_pair(blocks)
+    lift_out = lift_out.reshape(-1, lon_count, 64)[:, blocks].reshape(lift_out.shape)
+    place = lon_index.astype(jnp.int32).reshape(1)
     row_order = jnp.arange(NLAT, dtype=jnp.int32).reshape(lat_count, PARTS, 2 * pairs)
     row_order = jnp.swapaxes(row_order, 0, 1).reshape(NLAT)
     table, quadrature = legendre_table(own_orders, row_order)
@@ -561,7 +581,10 @@
     pieces = []
     for part in range(PARTS):
         lifted = lift_part(part, pairs, picks, widened, weight, lift_in, lift_out)
-        spectra = dft_part(forward, swap(lifted, "lon"), own_scale[part])
+        if part:
+            lifted, _ = lax.optimization_barrier((lifted, arrived))
+        arrived = exchange(lifted, "lon")
+        spectra = dft_part(forward, arrived, own_scale[part])
         gathered = swap(spectra, "lat").reshape(NLAT // PARTS, per_band, 128)
         pieces.append(jnp.swapaxes(gathered, 0, 1))
     analysis = analysis_all(table, pieces)
@@ -574,7 +597,7 @@
         sent = jnp.swapaxes(synthesized[part], 0, 1)
         sent = sent.reshape(lat_count, 2 * pairs, per_band, 128)
         placed = inverse_part(inverse, swap(sent, "lat"))
-        grid_field = join_part(part, swap(placed, "lon"), grid_field)
+        grid_field = join_part(part, place, exchange(placed, "lon"), grid_field)
     return grid_field
 
 

time: 1070 us -> 925 us (0.86)
  waiting for transfers between devices: 569 us -> 433 us
  starting transfers between devices: 59.5 us -> 41.9 us
    all_to_all x12 -> x6, waiting for transfers between devices: 559 us -> 176 us  [swap(): return lax.all_to_all(values, axis, split_axis=0, concat_axis=0, tiled=True)]
    ppermute x0 -> x18, waiting for transfers between devices: none -> 249 us  [exchange(): lax.ppermute(pieces[s], axis, [(i, i ^ s) for i in range(count)])]
    all_to_all x12 -> x6, starting transfers between devices: 57 us -> 28 us  [swap(): return lax.all_to_all(values, axis, split_axis=0, concat_axis=0, tiled=True)]
    ppermute x0 -> x18, starting transfers between devices: none -> 11.4 us  [exchange(): lax.ppermute(pieces[s], axis, [(i, i ^ s) for i in range(count)])]
  transfers between devices with their start and end apart: 14 -> 26, of which waited for: 14 -> 17; matrix products, arithmetic and copies ran while one was open for 5% -> 6% of each run, Pallas kernels for 16% -> 17%
where the time goes in v2:
time: 925 us; the launch traced here: 920 us
  waiting for transfers between devices  433 us (47%)
  Pallas kernels  251 us (27%)
  blocking collectives  115 us (12%)
  local copies, waits for them, and re-layouts  64.3 us (7%)
  starting transfers between devices  41.9 us (5%)
  other arithmetic  15.4 us (2%)
    ppermute x18, waiting for transfers between devices, exchange(): lax.ppermute(pieces[s], axis, [(i, i ^ s) for i in range(count)])  249 us
    all_to_all x6, waiting for transfers between devices, swap(): return lax.all_to_all(values, axis, split_axis=0, concat_axis=0, tiled=True)  176 us
    all_to_all x2, blocking collectives, swap(): return lax.all_to_all(values, axis, split_axis=0, concat_axis=0, tiled=True)  115 us
    pallas_call x3, Pallas kernels, lift_part(): pl.pallas_call(lambda *refs: lift_kernel(part * pairs * 2, *refs), out_sh...  62.9 us
    pallas_call x1, Pallas kernels, legendre_table(): pl.pallas_call(legendre_kernel, out_shape=jax.ShapeDtypeStruct((count, L,...  36.6 us
    pallas_call x3, Pallas kernels, join_part(): pl.pallas_call(join_kernel, out_shape=jax.ShapeDtypeStruct((2 * pairs * P...  35.1 us
    pallas_call x3, Pallas kernels, dft_part(): pl.pallas_call(dft_kernel, out_shape=jax.ShapeDtypeStruct((8, 2 * pairs,...  34.8 us
    pallas_call x3, Pallas kernels, inverse_part(): pl.pallas_call(inverse_kernel, out_shape=[jax.ShapeDtypeStruct((rows // 2...  29.3 us
  transfers between devices with their start and end apart: 26, of which 17 were waited for; matrix products, arithmetic and copies ran while one was open for 6% of the time, Pallas kernels for 17%

profile of v2, /device:TPU:0, one launch (start us, length us, event | category | flops | bytes accessed | tf_op | source)
XLA Modules:
  0.0 920.3 jit_solution(18372874045443871885)
XLA Ops:
  1.8 2.0 collective-permute-start.1
  7.8 5.1 collective-permute-done
  13.1 2.3 collective-permute-done.1
  16.7 21.0 %lift_rows.3 = (bf16[15,360,128]{2,1,0:T(8,128)(2,1)}, bf16[15,360,128]{2,1,0:T(8,128)(2,1)}, bf16[15,360,128]{2,1,0:T(8,128)(2,1)}, bf16[15,360,128]{2,1,0:T(8,128)(2,1)}) custom-call(s32[360]{0:T(512)} %add_select_fusion.1.refs_0_, bf16[96,80,128]{2,1,0:T(8,128)(2,1)} %copy-done, bf16[90,4,360,128]{3,2,1,0:T(8,128)(2,1)} %bitcast.38, ...), custom_call_target="tpu_custom_call" | custom-call | flops 2831155200 | bytes 16588800 | tf_op jit(solution)/shard_map/lift_rows/pallas_call | solution.py:271
  37.9 2.4 collective-permute-start.3
  40.6 10.4 %cosine_convert_fusion = (bf16[4,384,360]{1,2,0:T(8,128)(2,1)S(1)}, bf16[4,384,360]{1,2,0:T(8,128)(2,1)S(1)}) fusion(s32[4,360]{1,0:T(4,128)S(1)} %iota_add_fusion), kind=kLoop, calls=%fused_computation.13 | loop fusion | flops 6635520 | bytes 2217600 | tf_op jit(solution)/shard_map/convert
  50.9 2.0 pad_maximum_fusion
  52.9 2.5 copy.47.table
  56.4 15.4 %collective-permute-done.3.third = bf16[15,360,128]{2,1,0:T(8,128)(2,1)} collective-permute-done((bf16[15,360,128]{2,1,0:T(8,128)(2,1)}, bf16[15,360,128]{2,1,0:T(8,128)(2,1)}, u32[]{:S(2)}, u32[]{:S(2)}) %collective-permute-start.3) | collective-permute-done | bytes 1382432 | tf_op jit(solution)/shard_map/ppermute | solution.py:536
  71.9 29.1 %collective-permute-done.4.fourth = bf16[15,360,128]{2,1,0:T(8,128)(2,1)} collective-permute-done((bf16[15,360,128]{2,1,0:T(8,128)(2,1)}, bf16[15,360,128]{2,1,0:T(8,128)(2,1)}, u32[]{:S(2)}, u32[]{:S(2)}) %collective-permute-start.4) | collective-permute-done | bytes 1382432 | tf_op jit(solution)/shard_map/ppermute | solution.py:536
  100.9 11.6 %forward_rows.3 = bf16[8,30,48,128]{3,2,1,0:T(8,128)(2,1)} custom-call(bf16[4,768,360]{2,1,0:T(8,128)(2,1)} %copy.47.table, f32[5,1,384]{2,1,0:T(1,128)} %broadcast_in_dim.41.scale, bf16[15,360,128]{2,1,0:T(8,128)(2,1)} %get-tuple-element.40.first, bf16[15,360,128]{2,1,0:T(8,128)(2,1)} %collective-permute-done.2.second, ...), custom_call_target="tpu_custom_call" | custom-call | flops 4246732800 | bytes 11059200 | tf_op jit(solution)/shard_map/forward_rows/pallas_call | solution.py:311
  112.5 4.8 all-to-all-start
  117.3 21.0 %lift_rows.4 = (bf16[15,360,128]{2,1,0:T(8,128)(2,1)}, bf16[15,360,128]{2,1,0:T(8,128)(2,1)}, bf16[15,360,128]{2,1,0:T(8,128)(2,1)}, bf16[15,360,128]{2,1,0:T(8,128)(2,1)}) custom-call(s32[360]{0:T(512)} %add_select_fusion.1.refs_0_, bf16[96,80,128]{2,1,0:T(8,128)(2,1)} %copy-done, bf16[90,4,360,128]{3,2,1,0:T(8,128)(2,1)} %bitcast.39, ...), custom_call_target="tpu_custom_call" | custom-call | flops 2831155200 | bytes 16588800 | tf_op jit(solution)/shard_map/lift_rows/pallas_call | solution.py:271
  138.7 1.5 collective-permute-start.6
  141.8 30.4 %collective-permute-done.6.third = bf16[15,360,128]{2,1,0:T(8,128)(2,1)} collective-permute-done((bf16[15,360,128]{2,1,0:T(8,128)(2,1)}, bf16[15,360,128]{2,1,0:T(8,128)(2,1)}, u32[]{:S(2)}, u32[]{:S(2)}) %collective-permute-start.6) | collective-permute-done | bytes 1382432 | tf_op jit(solution)/shard_map/ppermute | solution.py:536
  172.2 27.9 %collective-permute-done.7.fourth = bf16[15,360,128]{2,1,0:T(8,128)(2,1)} collective-permute-done((bf16[15,360,128]{2,1,0:T(8,128)(2,1)}, bf16[15,360,128]{2,1,0:T(8,128)(2,1)}, u32[]{:S(2)}, u32[]{:S(2)}) %collective-permute-start.7) | collective-permute-done | bytes 1382432 | tf_op jit(solution)/shard_map/ppermute | solution.py:536
  200.1 11.6 %forward_rows.4 = bf16[8,30,48,128]{3,2,1,0:T(8,128)(2,1)} custom-call(bf16[4,768,360]{2,1,0:T(8,128)(2,1)} %copy.47.table, f32[5,1,384]{2,1,0:T(1,128)} %broadcast_in_dim.44.scale, bf16[15,360,128]{2,1,0:T(8,128)(2,1)} %get-tuple-element.48.first, bf16[15,360,128]{2,1,0:T(8,128)(2,1)} %collective-permute-done.5.second, ...), custom_call_target="tpu_custom_call" | custom-call | flops 4246732800 | bytes 11059200 | tf_op jit(solution)/shard_map/forward_rows/pallas_call | solution.py:311
  211.7 6.3 all-to-all-start.1
  218.0 21.0 %lift_rows.5 = (bf16[15,360,128]{2,1,0:T(8,128)(2,1)}, bf16[15,360,128]{2,1,0:T(8,128)(2,1)}, bf16[15,360,128]{2,1,0:T(8,128)(2,1)}, bf16[15,360,128]{2,1,0:T(8,128)(2,1)}) custom-call(s32[360]{0:T(512)} %add_select_fusion.1.refs_0_, bf16[96,80,128]{2,1,0:T(8,128)(2,1)} %copy-done, bf16[90,4,360,128]{3,2,1,0:T(8,128)(2,1)} %bitcast.40, ...), custom_call_target="tpu_custom_call" | custom-call | flops 2831155200 | bytes 16588800 | tf_op jit(solution)/shard_map/lift_rows/pallas_call | solution.py:271
  242.0 29.7 %collective-permute-done.10.fourth = bf16[15,360,128]{2,1,0:T(8,128)(2,1)} collective-permute-done((bf16[15,360,128]{2,1,0:T(8,128)(2,1)}, bf16[15,360,128]{2,1,0:T(8,128)(2,1)}, u32[]{:S(2)}, u32[]{:S(2)}) %collective-permute-start.10) | collective-permute-done | bytes 1382432 | tf_op jit(solution)/shard_map/ppermute | solution.py:536
  271.7 29.9 %collective-permute-done.9.third = bf16[15,360,128]{2,1,0:T(8,128)(2,1)} collective-permute-done((bf16[15,360,128]{2,1,0:T(8,128)(2,1)}, bf16[15,360,128]{2,1,0:T(8,128)(2,1)}, u32[]{:S(2)}, u32[]{:S(2)}) %collective-permute-start.9) | collective-permute-done | bytes 1382432 | tf_op jit(solution)/shard_map/ppermute | solution.py:536
  301.6 11.6 %forward_rows.5 = bf16[8,30,48,128]{3,2,1,0:T(8,128)(2,1)} custom-call(bf16[4,768,360]{2,1,0:T(8,128)(2,1)} %copy.47.table, f32[5,1,384]{2,1,0:T(1,128)} %broadcast_in_dim.47.scale, bf16[15,360,128]{2,1,0:T(8,128)(2,1)} %get-tuple-element.56.first, bf16[15,360,128]{2,1,0:T(8,128)(2,1)} %collective-permute-done.8.second, ...), custom_call_target="tpu_custom_call" | custom-call | flops 4246732800 | bytes 11059200 | tf_op jit(solution)/shard_map/forward_rows/pallas_call | solution.py:311
  313.2 6.0 all-to-all-start.2
  321.2 2.3 gather_fusion.1
  323.4 1.8 copy.41
  325.4 2.3 gather_fusion.2
  328.7 1.6 pad.12.initial
  331.1 3.2 gather_fusion
  335.5 36.6 %legendre_table.1.table = bf16[48,384,720]{2,1,0:T(8,128)(2,1)} custom-call(f32[1,768]{1,0:T(1,128)} %pad.11.cosine, f32[48,1]{1,0:T(8,128)} %add_convert_fusion.order, f32[48,768]{1,0:T(8,128)} %pad.12.initial, f32[48,768]{1,0:T(8,128)} %pad.13.restore), custom_call_target="tpu_custom_call" | custom-call | flops 1415577600 | bytes 26542080 | tf_op jit(solution)/shard_map/legendre_table/pallas_call | solution.py:366
  372.2 2.4 copy.65
  374.6 4.2 copy.64
  378.7 7.2 all-to-all-done.2
  386.0 4.2 copy.63
  390.2 19.0 %analysis.1 = bf16[48,384,128]{2,1,0:T(8,128)(2,1)} custom-call(bf16[48,384,720]{2,1,0:T(8,128)(2,1)} %legendre_table.1.table, bf16[48,240,128]{2,1,0:T(8,128)(2,1)} %bitcast.44, bf16[48,240,128]{2,1,0:T(8,128)(2,1)} %bitcast.45, bf16[48,240,128]{2,1,0:T(8,128)(2,1)} %bitcast.46), custom_call_target="tpu_custom_call" | custom-call | flops 3397386240 | bytes 26542080 | tf_op jit(solution)/shard_map/analysis/pallas_call | solution.py:398
  409.2 5.4 copy.55
  414.5 57.3 %all_to_all.40.data = bf16[4,96,48,128]{3,2,1,0:T(8,128)(2,1)} all-to-all(bf16[4,96,48,128]{3,2,1,0:T(8,128)(2,1)S(1)} %bitcast.41), channel_id=1, replica_groups=mesh['lat'=8,'lon'=4] {'lon'}, dimensions={0} | all-to-all | bytes 9437184 | tf_op jit(solution)/shard_map/all_to_all | solution.py:542
  471.9 13.3 %mixing.1 = bf16[4,96,48,128]{3,2,1,0:T(8,128)(2,1)} custom-call(bf16[4,96,48,128]{3,2,1,0:T(8,128)(2,1)} %all_to_all.40.data, bf16[96,256,256]{2,1,0:T(8,128)(2,1)} %matrix.1), custom_call_target="tpu_custom_call" | custom-call | flops 1207959552 | bytes 12582912 | tf_op jit(solution)/shard_map/mixing/pallas_call | solution.py:428
  485.1 57.6 %all_to_all.41 = bf16[4,96,48,128]{3,2,1,0:T(8,128)(2,1)S(1)} all-to-all(bf16[4,96,48,128]{3,2,1,0:T(8,128)(2,1)} %mixing.1), channel_id=1, replica_groups=mesh['lat'=8,'lon'=4] {'lon'}, dimensions={0} | all-to-all | bytes 9437184 | tf_op jit(solution)/shard_map/all_to_all | solution.py:542
  542.7 3.4 copy.56
  546.1 19.6 %synthesis.1 = (bf16[48,240,128]{2,1,0:T(8,128)(2,1)}, bf16[48,240,128]{2,1,0:T(8,128)(2,1)}, bf16[48,240,128]{2,1,0:T(8,128)(2,1)}) custom-call(bf16[48,384,720]{2,1,0:T(8,128)(2,1)} %legendre_table.1.table, bf16[48,384,128]{2,1,0:T(8,128)(2,1)} %bitcast.42), custom_call_target="tpu_custom_call" | custom-call | flops 3397386240 | bytes 26542080 | tf_op jit(solution)/shard_map/synthesis/pallas_call | solution.py:454
  565.7 4.2 copy.59
  569.9 3.6 all-to-all-start.7
  573.6 4.2 copy.58
  577.7 62.2 %all-to-all-done.7.data = bf16[8,30,48,128]{3,2,1,0:T(8,128)(2,1)S(1)} async-done(((bf16[8,30,48,128]{3,2,1,0:T(8,128)(2,1)}), bf16[8,30,48,128]{3,2,1,0:T(8,128)(2,1)S(1)}, u32[]{:S(2)}, u32[]{:S(2)}) %all-to-all-start.7) | async-done | bytes 2949152 | tf_op jit(solution)/shard_map/all_to_all | solution.py:542
  639.9 1.6 copy-done.4
  641.5 3.6 all-to-all-start.6
  645.1 4.2 copy.57
  649.3 62.5 %all-to-all-done.6.data = bf16[8,30,48,128]{3,2,1,0:T(8,128)(2,1)S(1)} async-done(((bf16[8,30,48,128]{3,2,1,0:T(8,128)(2,1)}), bf16[8,30,48,128]{3,2,1,0:T(8,128)(2,1)S(1)}, u32[]{:S(2)}, u32[]{:S(2)}) %all-to-all-start.6) | async-done | bytes 2949152 | tf_op jit(solution)/shard_map/all_to_all | solution.py:542
  711.8 1.6 copy-done.3
  713.4 3.6 all-to-all-start.5
  717.0 9.8 %inverse_rows.5 = (bf16[15,360,128]{2,1,0:T(8,128)(2,1)}, bf16[15,360,128]{2,1,0:T(8,128)(2,1)}, bf16[15,360,128]{2,1,0:T(8,128)(2,1)}, bf16[15,360,128]{2,1,0:T(8,128)(2,1)}) custom-call(bf16[4,360,768]{2,1,0:T(8,128)(2,1)} %get-tuple-element.76.table, bf16[8,30,48,128]{3,2,1,0:T(8,128)(2,1)} %copy-done.4), custom_call_target="tpu_custom_call" | custom-call | flops 4246732800 | bytes 11059200 | tf_op jit(solution)/shard_map/inverse_rows/pallas_call | solution.py:485
  727.2 1.5 collective-permute-start.19
  728.7 9.8 %inverse_rows.4 = (bf16[15,360,128]{2,1,0:T(8,128)(2,1)}, bf16[15,360,128]{2,1,0:T(8,128)(2,1)}, bf16[15,360,128]{2,1,0:T(8,128)(2,1)}, bf16[15,360,128]{2,1,0:T(8,128)(2,1)}) custom-call(bf16[4,360,768]{2,1,0:T(8,128)(2,1)} %get-tuple-element.76.table, bf16[8,30,48,128]{3,2,1,0:T(8,128)(2,1)} %copy-done.3), custom_call_target="tpu_custom_call" | custom-call | flops 4246732800 | bytes 11059200 | tf_op jit(solution)/shard_map/inverse_rows/pallas_call | solution.py:485
  739.1 44.6 %all-to-all-done.5.data = bf16[8,30,48,128]{3,2,1,0:T(8,128)(2,1)S(1)} async-done(((bf16[8,30,48,128]{3,2,1,0:T(8,128)(2,1)}), bf16[8,30,48,128]{3,2,1,0:T(8,128)(2,1)S(1)}, u32[]{:S(2)}, u32[]{:S(2)}) %all-to-all-start.5) | async-done | bytes 2949152 | tf_op jit(solution)/shard_map/all_to_all | solution.py:542
  783.7 1.6 copy-done.2
  785.3 9.8 %inverse_rows.3 = (bf16[15,360,128]{2,1,0:T(8,128)(2,1)}, bf16[15,360,128]{2,1,0:T(8,128)(2,1)}, bf16[15,360,128]{2,1,0:T(8,128)(2,1)}, bf16[15,360,128]{2,1,0:T(8,128)(2,1)}) custom-call(bf16[4,360,768]{2,1,0:T(8,128)(2,1)} %get-tuple-element.76.table, bf16[8,30,48,128]{3,2,1,0:T(8,128)(2,1)} %copy-done.2), custom_call_target="tpu_custom_call" | custom-call | flops 4246732800 | bytes 11059200 | tf_op jit(solution)/shard_map/inverse_rows/pallas_call | solution.py:485
  795.5 1.7 collective-permute-start.12
  797.2 11.7 %join_rows.3.refs_4_ = bf16[90,360,256]{2,1,0:T(8,128)(2,1)} custom-call(s32[1]{0:T(128)} %bitcast.place, bf16[15,360,128]{2,1,0:T(8,128)(2,1)} %get-tuple-element.71.refs_0_, bf16[15,360,128]{2,1,0:T(8,128)(2,1)} %collective-permute-done.17.refs_1_, bf16[15,360,128]{2,1,0:T(8,128)(2,1)} %collective-permute-done.18.refs_2_, ...), custom_call_target="tpu_custom_call" | custom-call | bytes 11059200 | tf_op jit(solution)/shard_map/join_rows/pallas_call | solution.py:516
  808.9 10.6 %collective-permute-done.15.refs_2_ = bf16[15,360,128]{2,1,0:T(8,128)(2,1)} collective-permute-done((bf16[15,360,128]{2,1,0:T(8,128)(2,1)}, bf16[15,360,128]{2,1,0:T(8,128)(2,1)}, u32[]{:S(2)}, u32[]{:S(2)}) %collective-permute-start.15) | collective-permute-done | bytes 1382432 | tf_op jit(solution)/shard_map/ppermute | solution.py:536
  819.5 28.7 %collective-permute-done.16.refs_3_ = bf16[15,360,128]{2,1,0:T(8,128)(2,1)S(1)} collective-permute-done((bf16[15,360,128]{2,1,0:T(8,128)(2,1)}, bf16[15,360,128]{2,1,0:T(8,128)(2,1)S(1)}, u32[]{:S(2)}, u32[]{:S(2)}) %collective-permute-start.16) | collective-permute-done | bytes 1382432 | tf_op jit(solution)/shard_map/ppermute | solution.py:536
  849.3 11.7 %join_rows.4.refs_4_ = bf16[90,360,256]{2,1,0:T(8,128)(2,1)} custom-call(s32[1]{0:T(128)} %bitcast.place, bf16[15,360,128]{2,1,0:T(8,128)(2,1)} %get-tuple-element.66.refs_0_, bf16[15,360,128]{2,1,0:T(8,128)(2,1)} %collective-permute-done.14.refs_1_, bf16[15,360,128]{2,1,0:T(8,128)(2,1)} %collective-permute-done.15.refs_2_, ...), custom_call_target="tpu_custom_call", output_to_operand_aliasing={{}: (5, {})} | custom-call | bytes 11059200 | tf_op jit(solution)/shard_map/join_rows/pallas_call | solution.py:516
  861.0 17.6 %collective-permute-done.12.refs_2_ = bf16[15,360,128]{2,1,0:T(8,128)(2,1)S(1)} collective-permute-done((bf16[15,360,128]{2,1,0:T(8,128)(2,1)}, bf16[15,360,128]{2,1,0:T(8,128)(2,1)S(1)}, u32[]{:S(2)}, u32[]{:S(2)}) %collective-permute-start.12) | collective-permute-done | bytes 1382432 | tf_op jit(solution)/shard_map/ppermute | solution.py:536
  878.6 28.8 %collective-permute-done.13.refs_3_ = bf16[15,360,128]{2,1,0:T(8,128)(2,1)S(1)} collective-permute-done((bf16[15,360,128]{2,1,0:T(8,128)(2,1)}, bf16[15,360,128]{2,1,0:T(8,128)(2,1)S(1)}, u32[]{:S(2)}, u32[]{:S(2)}) %collective-permute-start.13) | collective-permute-done | bytes 1382432 | tf_op jit(solution)/shard_map/ppermute | solution.py:536
  908.6 11.7 %join_rows.5 = bf16[90,360,256]{2,1,0:T(8,128)(2,1)} custom-call(s32[1]{0:T(128)} %bitcast.place, bf16[15,360,128]{2,1,0:T(8,128)(2,1)} %get-tuple-element.61.refs_0_, bf16[15,360,128]{2,1,0:T(8,128)(2,1)} %copy-done.5, bf16[15,360,128]{2,1,0:T(8,128)(2,1)} %copy-done.6, bf16[15,360,128]{2,1,0:T(8,128)(2,1)} %copy-done.8, ...), custom_call_target="tpu_custom_call", output_to_operand_aliasing={{}: (5, {})} | custom-call | bytes 11059200 | tf_op jit(solution)/shard_map/join_rows/pallas_call | solution.py:516
  (85 shorter events, 22.6 us)
Async XLA Ops:
  0.0 12.9 %copy-start.1 = (bf16[48,80,128]{2,1,0:T(8,128)(2,1)S(1)}, bf16[48,80,128]{2,1,0:T(8,128)(2,1)}, u32[]{:S(2)}) copy-start(bf16[48,80,128]{2,1,0:T(8,128)(2,1)} %param.6) | copy-start | bytes 2949124
  1.3 11.5 %collective-permute-start = (bf16[24,80,128]{2,1,0:T(8,128)(2,1)S(1)}, bf16[24,80,128]{2,1,0:T(8,128)(2,1)S(1)}, u32[]{:S(2)}, u32[]{:S(2)}) collective-permute-start(bf16[24,80,128]{2,1,0:T(8,128)(2,1)S(1)} %get-tuple-element.78), channel_id=1, source_target_pairs={{0,1},{1,2},{2,3},{3,0},{4,5},{5,6},{6,7},{7,4},{8,9},{9,10},{10,1... | collective-permute-start | bytes 1474568 | tf_op jit(solution)/shard_map/ppermute | solution.py:26
  1.8 13.5 %collective-permute-start.1 = (bf16[24,80,128]{2,1,0:T(8,128)(2,1)S(1)}, bf16[24,80,128]{2,1,0:T(8,128)(2,1)S(1)}, u32[]{:S(2)}, u32[]{:S(2)}) collective-permute-start(bf16[24,80,128]{2,1,0:T(8,128)(2,1)S(1)} %get-tuple-element.77), channel_id=1, source_target_pairs={{1,0},{2,1},{3,2},{0,3},{5,4},{6,5},{7,6},{4,7},{9,8},{10,9},{11,1... | collective-permute-start | bytes 1474568 | tf_op jit(solution)/shard_map/ppermute | solution.py:28
  15.4 1.3 copy-start
  37.7 18.8 %collective-permute-start.2 = (bf16[15,360,128]{2,1,0:T(8,128)(2,1)}, bf16[15,360,128]{2,1,0:T(8,128)(2,1)}, u32[]{:S(2)}, u32[]{:S(2)}) collective-permute-start(bf16[15,360,128]{2,1,0:T(8,128)(2,1)} %get-tuple-element.41), channel_id=1, source_target_pairs={{0,1},{1,0},{2,3},{3,2},{4,5},{5,4},{6,7},{7,6},{8,9},{9,8},{10,11... | collective-permute-start | bytes 4147208 | tf_op jit(solution)/shard_map/ppermute | solution.py:536
  37.9 33.9 %collective-permute-start.3 = (bf16[15,360,128]{2,1,0:T(8,128)(2,1)}, bf16[15,360,128]{2,1,0:T(8,128)(2,1)}, u32[]{:S(2)}, u32[]{:S(2)}) collective-permute-start(bf16[15,360,128]{2,1,0:T(8,128)(2,1)} %get-tuple-element.42), channel_id=1, source_target_pairs={{0,2},{1,3},{2,0},{3,1},{4,6},{5,7},{6,4},{7,5},{8,10},{9,11},{10,... | collective-permute-start | bytes 4147208 | tf_op jit(solution)/shard_map/ppermute | solution.py:536
  40.4 60.6 %collective-permute-start.4 = (bf16[15,360,128]{2,1,0:T(8,128)(2,1)}, bf16[15,360,128]{2,1,0:T(8,128)(2,1)}, u32[]{:S(2)}, u32[]{:S(2)}) collective-permute-start(bf16[15,360,128]{2,1,0:T(8,128)(2,1)} %get-tuple-element.43), channel_id=1, source_target_pairs={{0,3},{1,2},{2,1},{3,0},{4,7},{5,6},{6,5},{7,4},{8,11},{9,10},{10,... | collective-permute-start | bytes 4147208 | tf_op jit(solution)/shard_map/ppermute | solution.py:536
  112.5 99.2 %all-to-all-start = ((bf16[8,30,48,128]{3,2,1,0:T(8,128)(2,1)}), bf16[8,30,48,128]{3,2,1,0:T(8,128)(2,1)S(1)}, u32[]{:S(2)}, u32[]{:S(2)}) async-start(bf16[8,30,48,128]{3,2,1,0:T(8,128)(2,1)} %forward_rows.3), calls=%async_computation | async-start | bytes 5898240 | tf_op jit(solution)/shard_map/all_to_all | solution.py:542
  138.3 3.5 collective-permute-start.5
  138.7 33.5 %collective-permute-start.6 = (bf16[15,360,128]{2,1,0:T(8,128)(2,1)}, bf16[15,360,128]{2,1,0:T(8,128)(2,1)}, u32[]{:S(2)}, u32[]{:S(2)}) collective-permute-start(bf16[15,360,128]{2,1,0:T(8,128)(2,1)} %get-tuple-element.50), channel_id=1, source_target_pairs={{0,2},{1,3},{2,0},{3,1},{4,6},{5,7},{6,4},{7,5},{8,10},{9,11},{10,... | collective-permute-start | bytes 4147208 | tf_op jit(solution)/shard_map/ppermute | solution.py:536
  140.2 59.9 %collective-permute-start.7 = (bf16[15,360,128]{2,1,0:T(8,128)(2,1)}, bf16[15,360,128]{2,1,0:T(8,128)(2,1)}, u32[]{:S(2)}, u32[]{:S(2)}) collective-permute-start(bf16[15,360,128]{2,1,0:T(8,128)(2,1)} %get-tuple-element.51), channel_id=1, source_target_pairs={{0,3},{1,2},{2,1},{3,0},{4,7},{5,6},{6,5},{7,4},{8,11},{9,10},{10,... | collective-permute-start | bytes 4147208 | tf_op jit(solution)/shard_map/ppermute | solution.py:536
  211.7 101.4 %all-to-all-start.1 = ((bf16[8,30,48,128]{3,2,1,0:T(8,128)(2,1)}), bf16[8,30,48,128]{3,2,1,0:T(8,128)(2,1)}, u32[]{:S(2)}, u32[]{:S(2)}) async-start(bf16[8,30,48,128]{3,2,1,0:T(8,128)(2,1)} %forward_rows.4), calls=%async_computation.1 | async-start | bytes 5898240 | tf_op jit(solution)/shard_map/all_to_all | solution.py:542
  239.0 32.7 %collective-permute-start.10 = (bf16[15,360,128]{2,1,0:T(8,128)(2,1)}, bf16[15,360,128]{2,1,0:T(8,128)(2,1)}, u32[]{:S(2)}, u32[]{:S(2)}) collective-permute-start(bf16[15,360,128]{2,1,0:T(8,128)(2,1)} %get-tuple-element.59), channel_id=1, source_target_pairs={{0,3},{1,2},{2,1},{3,0},{4,7},{5,6},{6,5},{7,4},{8,11},{9,10},{10,... | collective-permute-start | bytes 4147208 | tf_op jit(solution)/shard_map/ppermute | solution.py:536
  240.2 31.5 %collective-permute-start.8 = (bf16[15,360,128]{2,1,0:T(8,128)(2,1)}, bf16[15,360,128]{2,1,0:T(8,128)(2,1)}, u32[]{:S(2)}, u32[]{:S(2)}) collective-permute-start(bf16[15,360,128]{2,1,0:T(8,128)(2,1)} %get-tuple-element.57), channel_id=1, source_target_pairs={{0,1},{1,0},{2,3},{3,2},{4,5},{5,4},{6,7},{7,6},{8,9},{9,8},{10,11... | collective-permute-start | bytes 4147208 | tf_op jit(solution)/shard_map/ppermute | solution.py:536
  240.6 61.0 %collective-permute-start.9 = (bf16[15,360,128]{2,1,0:T(8,128)(2,1)}, bf16[15,360,128]{2,1,0:T(8,128)(2,1)}, u32[]{:S(2)}, u32[]{:S(2)}) collective-permute-start(bf16[15,360,128]{2,1,0:T(8,128)(2,1)} %get-tuple-element.58), channel_id=1, source_target_pairs={{0,2},{1,3},{2,0},{3,1},{4,6},{5,7},{6,4},{7,5},{8,10},{9,11},{10,... | collective-permute-start | bytes 4147208 | tf_op jit(solution)/shard_map/ppermute | solution.py:536
  313.2 72.8 %all-to-all-start.2 = ((bf16[8,30,48,128]{3,2,1,0:T(8,128)(2,1)}), bf16[8,30,48,128]{3,2,1,0:T(8,128)(2,1)}, u32[]{:S(2)}, u32[]{:S(2)}) async-start(bf16[8,30,48,128]{3,2,1,0:T(8,128)(2,1)} %forward_rows.5), calls=%async_computation.2 | async-start | bytes 5898240 | tf_op jit(solution)/shard_map/all_to_all | solution.py:542
  569.9 70.0 %all-to-all-start.7 = ((bf16[8,30,48,128]{3,2,1,0:T(8,128)(2,1)}), bf16[8,30,48,128]{3,2,1,0:T(8,128)(2,1)S(1)}, u32[]{:S(2)}, u32[]{:S(2)}) async-start(bf16[8,30,48,128]{3,2,1,0:T(8,128)(2,1)} %bitcast.24), calls=%async_computation.7 | async-start | bytes 5898240 | tf_op jit(solution)/shard_map/all_to_all | solution.py:542
  639.9 1.6 copy-start.4
  641.5 70.3 %all-to-all-start.6 = ((bf16[8,30,48,128]{3,2,1,0:T(8,128)(2,1)}), bf16[8,30,48,128]{3,2,1,0:T(8,128)(2,1)S(1)}, u32[]{:S(2)}, u32[]{:S(2)}) async-start(bf16[8,30,48,128]{3,2,1,0:T(8,128)(2,1)} %bitcast.22), calls=%async_computation.6 | async-start | bytes 5898240 | tf_op jit(solution)/shard_map/all_to_all | solution.py:542
  711.8 1.6 copy-start.3
  713.4 70.3 %all-to-all-start.5 = ((bf16[8,30,48,128]{3,2,1,0:T(8,128)(2,1)}), bf16[8,30,48,128]{3,2,1,0:T(8,128)(2,1)S(1)}, u32[]{:S(2)}, u32[]{:S(2)}) async-start(bf16[8,30,48,128]{3,2,1,0:T(8,128)(2,1)} %bitcast.20), calls=%async_computation.5 | async-start | bytes 5898240 | tf_op jit(solution)/shard_map/all_to_all | solution.py:542
  726.8 68.2 %collective-permute-start.17 = (bf16[15,360,128]{2,1,0:T(8,128)(2,1)}, bf16[15,360,128]{2,1,0:T(8,128)(2,1)}, u32[]{:S(2)}, u32[]{:S(2)}) collective-permute-start(bf16[15,360,128]{2,1,0:T(8,128)(2,1)} %get-tuple-element.72), channel_id=1, source_target_pairs={{0,1},{1,0},{2,3},{3,2},{4,5},{5,4},{6,7},{7,6},{8,9},{9,8},{10,11... | collective-permute-start | bytes 4147208 | tf_op jit(solution)/shard_map/ppermute | solution.py:536
  726.8 68.2 %collective-permute-start.18 = (bf16[15,360,128]{2,1,0:T(8,128)(2,1)}, bf16[15,360,128]{2,1,0:T(8,128)(2,1)}, u32[]{:S(2)}, u32[]{:S(2)}) collective-permute-start(bf16[15,360,128]{2,1,0:T(8,128)(2,1)} %get-tuple-element.73), channel_id=1, source_target_pairs={{0,2},{1,3},{2,0},{3,1},{4,6},{5,7},{6,4},{7,5},{8,10},{9,11},{10,... | collective-permute-start | bytes 4147208 | tf_op jit(solution)/shard_map/ppermute | solution.py:536
  727.2 68.4 %collective-permute-start.19 = (bf16[15,360,128]{2,1,0:T(8,128)(2,1)}, bf16[15,360,128]{2,1,0:T(8,128)(2,1)}, u32[]{:S(2)}, u32[]{:S(2)}) collective-permute-start(bf16[15,360,128]{2,1,0:T(8,128)(2,1)} %get-tuple-element.74), channel_id=1, source_target_pairs={{0,3},{1,2},{2,1},{3,0},{4,7},{5,6},{6,5},{7,4},{8,11},{9,10},{10,... | collective-permute-start | bytes 4147208 | tf_op jit(solution)/shard_map/ppermute | solution.py:536
  738.4 58.8 %collective-permute-start.14 = (bf16[15,360,128]{2,1,0:T(8,128)(2,1)}, bf16[15,360,128]{2,1,0:T(8,128)(2,1)}, u32[]{:S(2)}, u32[]{:S(2)}) collective-permute-start(bf16[15,360,128]{2,1,0:T(8,128)(2,1)} %get-tuple-element.67), channel_id=1, source_target_pairs={{0,1},{1,0},{2,3},{3,2},{4,5},{5,4},{6,7},{7,6},{8,9},{9,8},{10,11... | collective-permute-start | bytes 4147208 | tf_op jit(solution)/shard_map/ppermute | solution.py:536
  738.7 80.8 %collective-permute-start.15 = (bf16[15,360,128]{2,1,0:T(8,128)(2,1)}, bf16[15,360,128]{2,1,0:T(8,128)(2,1)}, u32[]{:S(2)}, u32[]{:S(2)}) collective-permute-start(bf16[15,360,128]{2,1,0:T(8,128)(2,1)} %get-tuple-element.68), channel_id=1, source_target_pairs={{0,2},{1,3},{2,0},{3,1},{4,6},{5,7},{6,4},{7,5},{8,10},{9,11},{10,... | collective-permute-start | bytes 4147208 | tf_op jit(solution)/shard_map/ppermute | solution.py:536
  783.7 1.6 copy-start.2
  795.0 53.2 %collective-permute-start.16 = (bf16[15,360,128]{2,1,0:T(8,128)(2,1)}, bf16[15,360,128]{2,1,0:T(8,128)(2,1)S(1)}, u32[]{:S(2)}, u32[]{:S(2)}) collective-permute-start(bf16[15,360,128]{2,1,0:T(8,128)(2,1)} %get-tuple-element.69), channel_id=1, source_target_pairs={{0,3},{1,2},{2,1},{3,0},{4,7},{5,6},{6,5},{7,4},{8,11},{9,10},{10,... | collective-permute-start | bytes 4147208 | tf_op jit(solution)/shard_map/ppermute | solution.py:536
  795.1 66.0 %collective-permute-start.11 = (bf16[15,360,128]{2,1,0:T(8,128)(2,1)}, bf16[15,360,128]{2,1,0:T(8,128)(2,1)S(1)}, u32[]{:S(2)}, u32[]{:S(2)}) collective-permute-start(bf16[15,360,128]{2,1,0:T(8,128)(2,1)} %get-tuple-element.62), channel_id=1, source_target_pairs={{0,1},{1,0},{2,3},{3,2},{4,5},{5,4},{6,7},{7,6},{8,9},{9,8},{10,11... | collective-permute-start | bytes 4147208 | tf_op jit(solution)/shard_map/ppermute | solution.py:536
  795.5 83.1 %collective-permute-start.12 = (bf16[15,360,128]{2,1,0:T(8,128)(2,1)}, bf16[15,360,128]{2,1,0:T(8,128)(2,1)S(1)}, u32[]{:S(2)}, u32[]{:S(2)}) collective-permute-start(bf16[15,360,128]{2,1,0:T(8,128)(2,1)} %get-tuple-element.63), channel_id=1, source_target_pairs={{0,2},{1,3},{2,0},{3,1},{4,6},{5,7},{6,4},{7,5},{8,10},{9,11},{10,... | collective-permute-start | bytes 4147208 | tf_op jit(solution)/shard_map/ppermute | solution.py:536
  797.2 110.3 %collective-permute-start.13 = (bf16[15,360,128]{2,1,0:T(8,128)(2,1)}, bf16[15,360,128]{2,1,0:T(8,128)(2,1)S(1)}, u32[]{:S(2)}, u32[]{:S(2)}) collective-permute-start(bf16[15,360,128]{2,1,0:T(8,128)(2,1)} %get-tuple-element.64), channel_id=1, source_target_pairs={{0,3},{1,2},{2,1},{3,0},{4,7},{5,6},{6,5},{7,4},{8,11},{9,10},{10,... | collective-permute-start | bytes 4147208 | tf_op jit(solution)/shard_map/ppermute | solution.py:536
  848.2 1.1 copy-start.7
  861.0 46.5 %copy-start.5 = (bf16[15,360,128]{2,1,0:T(8,128)(2,1)}, bf16[15,360,128]{2,1,0:T(8,128)(2,1)S(1)}, u32[]{:S(2)}) copy-start(bf16[15,360,128]{2,1,0:T(8,128)(2,1)S(1)} %collective-permute-done.11.refs_1_) | copy-start | bytes 4147204
  878.6 28.9 %copy-start.6 = (bf16[15,360,128]{2,1,0:T(8,128)(2,1)}, bf16[15,360,128]{2,1,0:T(8,128)(2,1)S(1)}, u32[]{:S(2)}) copy-start(bf16[15,360,128]{2,1,0:T(8,128)(2,1)S(1)} %collective-permute-done.12.refs_2_) | copy-start | bytes 4147204
  907.5 1.1 copy-start.8

commit v3 on v2

--- a/solution.py
+++ b/solution.py
@@ -579,11 +579,12 @@
     own_scale = jnp.repeat(own_scale, 64).reshape(PARTS, pairs // PAIRS, 1, 128 * PAIRS)
 
     pieces = []
+    lifted = lift_part(0, pairs, picks, widened, weight, lift_in, lift_out)
     for part in range(PARTS):
-        lifted = lift_part(part, pairs, picks, widened, weight, lift_in, lift_out)
-        if part:
-            lifted, _ = lax.optimization_barrier((lifted, arrived))
         arrived = exchange(lifted, "lon")
+        if part + 1 < PARTS:
+            lifted = lift_part(part + 1, pairs, picks, widened, weight, lift_in, lift_out)
+            arrived, lifted = lax.optimization_barrier((arrived, lifted))
         spectra = dft_part(forward, arrived, own_scale[part])
         gathered = swap(spectra, "lat").reshape(NLAT // PARTS, per_band, 128)
         pieces.append(jnp.swapaxes(gathered, 0, 1))
@@ -593,10 +594,14 @@
     returned = swap(mix_all(by_degree, spectral), "lon").reshape(L, per_band, 128)
     synthesized = synthesis_all(table, jnp.swapaxes(returned, 0, 1))
     grid_field = None
+    ready = []
     for part in range(PARTS):
         sent = jnp.swapaxes(synthesized[part], 0, 1)
         sent = sent.reshape(lat_count, 2 * pairs, per_band, 128)
+        if part >= 2:
+            sent, _ = lax.optimization_barrier((sent, ready[part - 2]))
         placed = inverse_part(inverse, swap(sent, "lat"))
+        ready.append(placed)
         grid_field = join_part(part, place, exchange(placed, "lon"), grid_field)
     return grid_field
 

time: 925 us -> 875 us (0.946)
  waiting for transfers between devices: 433 us -> 386 us
    ppermute x18, waiting for transfers between devices: 249 us -> 199 us  [exchange(): lax.ppermute(pieces[s], axis, [(i, i ^ s) for i in range(count)])]
  transfers between devices with their start and end apart: 26 -> 26, of which waited for: 17 -> 15; matrix products, arithmetic and copies ran while one was open for 6% -> 6% of each run, Pallas kernels for 17% -> 18%
where the time goes in v3:
time: 875 us; the launch traced here: 870 us
  waiting for transfers between devices  386 us (44%)
  Pallas kernels  251 us (29%)
  blocking collectives  115 us (13%)
  local copies, waits for them, and re-layouts  59.3 us (7%)
  starting transfers between devices  42.6 us (5%)
  other arithmetic  15.5 us (2%)
    ppermute x18, waiting for transfers between devices, exchange(): lax.ppermute(pieces[s], axis, [(i, i ^ s) for i in range(count)])  199 us
    all_to_all x6, waiting for transfers between devices, swap(): return lax.all_to_all(values, axis, split_axis=0, concat_axis=0, tiled=True)  178 us
    all_to_all x2, blocking collectives, swap(): return lax.all_to_all(values, axis, split_axis=0, concat_axis=0, tiled=True)  115 us
    pallas_call x3, Pallas kernels, lift_part(): pl.pallas_call(lambda *refs: lift_kernel(part * pairs * 2, *refs), out_sh...  62.9 us
    pallas_call x1, Pallas kernels, legendre_table(): pl.pallas_call(legendre_kernel, out_shape=jax.ShapeDtypeStruct((count, L,...  36.6 us
    pallas_call x3, Pallas kernels, join_part(): pl.pallas_call(join_kernel, out_shape=jax.ShapeDtypeStruct((2 * pairs * P...  35.6 us
    pallas_call x3, Pallas kernels, dft_part(): pl.pallas_call(dft_kernel, out_shape=jax.ShapeDtypeStruct((8, 2 * pairs,...  34.8 us
    all_to_all x6, starting transfers between devices, swap(): return lax.all_to_all(values, axis, split_axis=0, concat_axis=0, tiled=True)  29.8 us
  transfers between devices with their start and end apart: 26, of which 15 were waited for; matrix products, arithmetic and copies ran while one was open for 6% of the time, Pallas kernels for 18%

profile of v3, /device:TPU:0, one launch (start us, length us, event | category | flops | bytes accessed | tf_op | source)
XLA Modules:
  0.0 870.0 jit_solution(8332530182093086744)
XLA Ops:
  0.0 1.3 fusion.16
  1.3 2.4 collective-permute-start.1
  7.0 9.4 %collective-permute-done = bf16[24,80,128]{2,1,0:T(8,128)(2,1)S(1)} collective-permute-done((bf16[24,80,128]{2,1,0:T(8,128)(2,1)S(1)}, bf16[24,80,128]{2,1,0:T(8,128)(2,1)S(1)}, u32[]{:S(2)}, u32[]{:S(2)}) %collective-permute-start) | collective-permute-done | bytes 491552 | tf_op jit(solution)/shard_map/ppermute | solution.py:26
  16.7 1.3 copy-done
  18.0 21.0 %lift_rows.3 = (bf16[15,360,128]{2,1,0:T(8,128)(2,1)}, bf16[15,360,128]{2,1,0:T(8,128)(2,1)}, bf16[15,360,128]{2,1,0:T(8,128)(2,1)}, bf16[15,360,128]{2,1,0:T(8,128)(2,1)}) custom-call(s32[360]{0:T(512)} %add_select_fusion.1.refs_0_, bf16[96,80,128]{2,1,0:T(8,128)(2,1)} %copy-done, bf16[90,4,360,128]{3,2,1,0:T(8,128)(2,1)} %bitcast.38, ...), custom_call_target="tpu_custom_call" | custom-call | flops 2831155200 | bytes 16588800 | tf_op jit(solution)/shard_map/lift_rows/pallas_call | solution.py:271
  39.0 1.5 collective-permute-start.3
  41.8 10.4 %cosine_convert_fusion = (bf16[4,384,360]{1,2,0:T(8,128)(2,1)S(1)}, bf16[4,384,360]{1,2,0:T(8,128)(2,1)S(1)}) fusion(s32[4,360]{1,0:T(4,128)S(1)} %iota_add_fusion), kind=kLoop, calls=%fused_computation.13 | loop fusion | flops 6635520 | bytes 2217600 | tf_op jit(solution)/shard_map/convert
  52.2 2.0 pad_maximum_fusion
  54.2 2.5 copy.48.table
  56.6 21.0 %lift_rows.4 = (bf16[15,360,128]{2,1,0:T(8,128)(2,1)}, bf16[15,360,128]{2,1,0:T(8,128)(2,1)}, bf16[15,360,128]{2,1,0:T(8,128)(2,1)}, bf16[15,360,128]{2,1,0:T(8,128)(2,1)}) custom-call(s32[360]{0:T(512)} %add_select_fusion.1.refs_0_, bf16[96,80,128]{2,1,0:T(8,128)(2,1)} %copy-done, bf16[90,4,360,128]{3,2,1,0:T(8,128)(2,1)} %bitcast.39, ...), custom_call_target="tpu_custom_call" | custom-call | flops 2831155200 | bytes 16588800 | tf_op jit(solution)/shard_map/lift_rows/pallas_call | solution.py:271
  77.6 23.6 %collective-permute-done.4.fourth = bf16[15,360,128]{2,1,0:T(8,128)(2,1)} collective-permute-done((bf16[15,360,128]{2,1,0:T(8,128)(2,1)}, bf16[15,360,128]{2,1,0:T(8,128)(2,1)}, u32[]{:S(2)}, u32[]{:S(2)}) %collective-permute-start.4) | collective-permute-done | bytes 1382432 | tf_op jit(solution)/shard_map/ppermute | solution.py:536
  101.2 11.6 %forward_rows.3 = bf16[8,30,48,128]{3,2,1,0:T(8,128)(2,1)} custom-call(bf16[4,768,360]{2,1,0:T(8,128)(2,1)} %copy.48.table, f32[5,1,384]{2,1,0:T(1,128)} %broadcast_in_dim.41.scale, bf16[15,360,128]{2,1,0:T(8,128)(2,1)} %get-tuple-element.57.first, bf16[15,360,128]{2,1,0:T(8,128)(2,1)} %collective-permute-done.2.second, ...), custom_call_target="tpu_custom_call" | custom-call | flops 4246732800 | bytes 11059200 | tf_op jit(solution)/shard_map/forward_rows/pallas_call | solution.py:311
  112.8 5.8 all-to-all-start
  118.6 1.5 collective-permute-start.6
  121.3 21.0 %lift_rows.5 = (bf16[15,360,128]{2,1,0:T(8,128)(2,1)}, bf16[15,360,128]{2,1,0:T(8,128)(2,1)}, bf16[15,360,128]{2,1,0:T(8,128)(2,1)}, bf16[15,360,128]{2,1,0:T(8,128)(2,1)}) custom-call(s32[360]{0:T(512)} %add_select_fusion.1.refs_0_, bf16[96,80,128]{2,1,0:T(8,128)(2,1)} %copy-done, bf16[90,4,360,128]{3,2,1,0:T(8,128)(2,1)} %bitcast.40, ...), custom_call_target="tpu_custom_call" | custom-call | flops 2831155200 | bytes 16588800 | tf_op jit(solution)/shard_map/lift_rows/pallas_call | solution.py:271
  142.3 9.8 %collective-permute-done.6.third = bf16[15,360,128]{2,1,0:T(8,128)(2,1)} collective-permute-done((bf16[15,360,128]{2,1,0:T(8,128)(2,1)}, bf16[15,360,128]{2,1,0:T(8,128)(2,1)}, u32[]{:S(2)}, u32[]{:S(2)}) %collective-permute-start.6) | collective-permute-done | bytes 1382432 | tf_op jit(solution)/shard_map/ppermute | solution.py:536
  152.1 28.7 %collective-permute-done.7.fourth = bf16[15,360,128]{2,1,0:T(8,128)(2,1)} collective-permute-done((bf16[15,360,128]{2,1,0:T(8,128)(2,1)}, bf16[15,360,128]{2,1,0:T(8,128)(2,1)}, u32[]{:S(2)}, u32[]{:S(2)}) %collective-permute-start.7) | collective-permute-done | bytes 1382432 | tf_op jit(solution)/shard_map/ppermute | solution.py:536
  180.8 11.6 %forward_rows.4 = bf16[8,30,48,128]{3,2,1,0:T(8,128)(2,1)} custom-call(bf16[4,768,360]{2,1,0:T(8,128)(2,1)} %copy.48.table, f32[5,1,384]{2,1,0:T(1,128)} %broadcast_in_dim.44.scale, bf16[15,360,128]{2,1,0:T(8,128)(2,1)} %get-tuple-element.69.first, bf16[15,360,128]{2,1,0:T(8,128)(2,1)} %collective-permute-done.5.second, ...), custom_call_target="tpu_custom_call" | custom-call | flops 4246732800 | bytes 11059200 | tf_op jit(solution)/shard_map/forward_rows/pallas_call | solution.py:311
  192.4 6.1 all-to-all-start.1
  198.6 1.5 collective-permute-start.9
  202.0 30.1 %collective-permute-done.9.third = bf16[15,360,128]{2,1,0:T(8,128)(2,1)} collective-permute-done((bf16[15,360,128]{2,1,0:T(8,128)(2,1)}, bf16[15,360,128]{2,1,0:T(8,128)(2,1)}, u32[]{:S(2)}, u32[]{:S(2)}) %collective-permute-start.9) | collective-permute-done | bytes 1382432 | tf_op jit(solution)/shard_map/ppermute | solution.py:536
  232.1 28.5 %collective-permute-done.10.fourth = bf16[15,360,128]{2,1,0:T(8,128)(2,1)} collective-permute-done((bf16[15,360,128]{2,1,0:T(8,128)(2,1)}, bf16[15,360,128]{2,1,0:T(8,128)(2,1)}, u32[]{:S(2)}, u32[]{:S(2)}) %collective-permute-start.10) | collective-permute-done | bytes 1382432 | tf_op jit(solution)/shard_map/ppermute | solution.py:536
  260.6 11.6 %forward_rows.5 = bf16[8,30,48,128]{3,2,1,0:T(8,128)(2,1)} custom-call(bf16[4,768,360]{2,1,0:T(8,128)(2,1)} %copy.48.table, f32[5,1,384]{2,1,0:T(1,128)} %broadcast_in_dim.47.scale, bf16[15,360,128]{2,1,0:T(8,128)(2,1)} %get-tuple-element.73.first, bf16[15,360,128]{2,1,0:T(8,128)(2,1)} %collective-permute-done.8.second, ...), custom_call_target="tpu_custom_call" | custom-call | flops 4246732800 | bytes 11059200 | tf_op jit(solution)/shard_map/forward_rows/pallas_call | solution.py:311
  272.2 6.2 all-to-all-start.2
  278.5 3.2 gather_fusion
  283.7 2.3 gather_fusion.2
  288.5 2.3 gather_fusion.1
  290.7 1.1 copy.41
  293.1 36.6 %legendre_table.1.table = bf16[48,384,720]{2,1,0:T(8,128)(2,1)} custom-call(f32[1,768]{1,0:T(1,128)} %pad.11.cosine, f32[48,1]{1,0:T(8,128)} %add_convert_fusion.order, f32[48,768]{1,0:T(8,128)} %pad.12.initial, f32[48,768]{1,0:T(8,128)} %pad.13.restore), custom_call_target="tpu_custom_call" | custom-call | flops 1415577600 | bytes 26542080 | tf_op jit(solution)/shard_map/legendre_table/pallas_call | solution.py:366
  329.7 2.4 copy.65
  332.1 4.2 copy.64
  336.3 9.3 %all-to-all-done.2 = bf16[8,30,48,128]{3,2,1,0:T(8,128)(2,1)} async-done(((bf16[8,30,48,128]{3,2,1,0:T(8,128)(2,1)}), bf16[8,30,48,128]{3,2,1,0:T(8,128)(2,1)}, u32[]{:S(2)}, u32[]{:S(2)}) %all-to-all-start.2) | async-done | bytes 2949152 | tf_op jit(solution)/shard_map/all_to_all | solution.py:542
  345.6 4.2 copy.63
  349.8 19.0 %analysis.1 = bf16[48,384,128]{2,1,0:T(8,128)(2,1)} custom-call(bf16[48,384,720]{2,1,0:T(8,128)(2,1)} %legendre_table.1.table, bf16[48,240,128]{2,1,0:T(8,128)(2,1)} %bitcast.44, bf16[48,240,128]{2,1,0:T(8,128)(2,1)} %bitcast.45, bf16[48,240,128]{2,1,0:T(8,128)(2,1)} %bitcast.46), custom_call_target="tpu_custom_call" | custom-call | flops 3397386240 | bytes 26542080 | tf_op jit(solution)/shard_map/analysis/pallas_call | solution.py:398
  368.8 5.4 copy.55
  374.2 57.3 %all_to_all.40.data = bf16[4,96,48,128]{3,2,1,0:T(8,128)(2,1)} all-to-all(bf16[4,96,48,128]{3,2,1,0:T(8,128)(2,1)S(1)} %bitcast.41), channel_id=1, replica_groups=mesh['lat'=8,'lon'=4] {'lon'}, dimensions={0} | all-to-all | bytes 9437184 | tf_op jit(solution)/shard_map/all_to_all | solution.py:542
  431.5 13.3 %mixing.1 = bf16[4,96,48,128]{3,2,1,0:T(8,128)(2,1)} custom-call(bf16[4,96,48,128]{3,2,1,0:T(8,128)(2,1)} %all_to_all.40.data, bf16[96,256,256]{2,1,0:T(8,128)(2,1)} %matrix.1), custom_call_target="tpu_custom_call" | custom-call | flops 1207959552 | bytes 12582912 | tf_op jit(solution)/shard_map/mixing/pallas_call | solution.py:428
  444.8 57.6 %all_to_all.41 = bf16[4,96,48,128]{3,2,1,0:T(8,128)(2,1)S(1)} all-to-all(bf16[4,96,48,128]{3,2,1,0:T(8,128)(2,1)} %mixing.1), channel_id=1, replica_groups=mesh['lat'=8,'lon'=4] {'lon'}, dimensions={0} | all-to-all | bytes 9437184 | tf_op jit(solution)/shard_map/all_to_all | solution.py:542
  502.4 3.4 copy.56
  505.8 19.6 %synthesis.1 = (bf16[48,240,128]{2,1,0:T(8,128)(2,1)}, bf16[48,240,128]{2,1,0:T(8,128)(2,1)}, bf16[48,240,128]{2,1,0:T(8,128)(2,1)}) custom-call(bf16[48,384,720]{2,1,0:T(8,128)(2,1)} %legendre_table.1.table, bf16[48,384,128]{2,1,0:T(8,128)(2,1)} %bitcast.42), custom_call_target="tpu_custom_call" | custom-call | flops 3397386240 | bytes 26542080 | tf_op jit(solution)/shard_map/synthesis/pallas_call | solution.py:454
  525.4 4.2 copy.58
  529.6 3.6 all-to-all-start.5
  533.2 4.2 copy.59
  537.4 62.2 %all-to-all-done.5.data = bf16[8,30,48,128]{3,2,1,0:T(8,128)(2,1)S(1)} async-done(((bf16[8,30,48,128]{3,2,1,0:T(8,128)(2,1)}), bf16[8,30,48,128]{3,2,1,0:T(8,128)(2,1)S(1)}, u32[]{:S(2)}, u32[]{:S(2)}) %all-to-all-start.5) | async-done | bytes 2949152 | tf_op jit(solution)/shard_map/all_to_all | solution.py:542
  599.5 1.6 copy-done.3
  601.1 3.6 all-to-all-start.7
  604.8 4.2 copy.57
  609.0 9.8 %inverse_rows.3 = (bf16[15,360,128]{2,1,0:T(8,128)(2,1)}, bf16[15,360,128]{2,1,0:T(8,128)(2,1)}, bf16[15,360,128]{2,1,0:T(8,128)(2,1)}, bf16[15,360,128]{2,1,0:T(8,128)(2,1)}) custom-call(bf16[4,360,768]{2,1,0:T(8,128)(2,1)} %get-tuple-element.94.table, bf16[8,30,48,128]{3,2,1,0:T(8,128)(2,1)} %copy-done.3), custom_call_target="tpu_custom_call" | custom-call | flops 4246732800 | bytes 11059200 | tf_op jit(solution)/shard_map/inverse_rows/pallas_call | solution.py:485
  618.8 52.7 %all-to-all-done.7.data = bf16[8,30,48,128]{3,2,1,0:T(8,128)(2,1)S(1)} async-done(((bf16[8,30,48,128]{3,2,1,0:T(8,128)(2,1)}), bf16[8,30,48,128]{3,2,1,0:T(8,128)(2,1)S(1)}, u32[]{:S(2)}, u32[]{:S(2)}) %all-to-all-start.7) | async-done | bytes 2949152 | tf_op jit(solution)/shard_map/all_to_all | solution.py:542
  671.4 1.6 copy-done.2
  673.0 4.4 all-to-all-start.6
  678.0 1.4 collective-permute-start.19
  679.4 9.8 %inverse_rows.5 = (bf16[15,360,128]{2,1,0:T(8,128)(2,1)}, bf16[15,360,128]{2,1,0:T(8,128)(2,1)}, bf16[15,360,128]{2,1,0:T(8,128)(2,1)}, bf16[15,360,128]{2,1,0:T(8,128)(2,1)}) custom-call(bf16[4,360,768]{2,1,0:T(8,128)(2,1)} %get-tuple-element.94.table, bf16[8,30,48,128]{3,2,1,0:T(8,128)(2,1)} %copy-done.2), custom_call_target="tpu_custom_call" | custom-call | flops 4246732800 | bytes 11059200 | tf_op jit(solution)/shard_map/inverse_rows/pallas_call | solution.py:485
  689.9 53.6 %all-to-all-done.6.data = bf16[8,30,48,128]{3,2,1,0:T(8,128)(2,1)} async-done(((bf16[8,30,48,128]{3,2,1,0:T(8,128)(2,1)}), bf16[8,30,48,128]{3,2,1,0:T(8,128)(2,1)}, u32[]{:S(2)}, u32[]{:S(2)}) %all-to-all-start.6) | async-done | bytes 2949152 | tf_op jit(solution)/shard_map/all_to_all | solution.py:542
  743.5 9.8 %inverse_rows.4 = (bf16[15,360,128]{2,1,0:T(8,128)(2,1)}, bf16[15,360,128]{2,1,0:T(8,128)(2,1)}, bf16[15,360,128]{2,1,0:T(8,128)(2,1)}, bf16[15,360,128]{2,1,0:T(8,128)(2,1)}) custom-call(bf16[4,360,768]{2,1,0:T(8,128)(2,1)} %get-tuple-element.94.table, bf16[8,30,48,128]{3,2,1,0:T(8,128)(2,1)} %all-to-all-done.6.data), custom_call_target="tpu_custom_call" | custom-call | flops 4246732800 | bytes 11059200 | tf_op jit(solution)/shard_map/inverse_rows/pallas_call | solution.py:485
  753.7 1.7 collective-permute-start.12
  755.4 12.2 %join_rows.3.refs_4_ = bf16[90,360,256]{2,1,0:T(8,128)(2,1)} custom-call(s32[1]{0:T(128)} %bitcast.place, bf16[15,360,128]{2,1,0:T(8,128)(2,1)} %get-tuple-element.79.refs_0_, bf16[15,360,128]{2,1,0:T(8,128)(2,1)} %collective-permute-done.17.refs_1_, bf16[15,360,128]{2,1,0:T(8,128)(2,1)} %collective-permute-done.18.refs_2_, ...), custom_call_target="tpu_custom_call" | custom-call | bytes 11059200 | tf_op jit(solution)/shard_map/join_rows/pallas_call | solution.py:516
  767.6 2.6 collective-permute-done.15.refs_2_
  770.2 28.7 %collective-permute-done.16.refs_3_ = bf16[15,360,128]{2,1,0:T(8,128)(2,1)S(1)} collective-permute-done((bf16[15,360,128]{2,1,0:T(8,128)(2,1)}, bf16[15,360,128]{2,1,0:T(8,128)(2,1)S(1)}, u32[]{:S(2)}, u32[]{:S(2)}) %collective-permute-start.16) | collective-permute-done | bytes 1382432 | tf_op jit(solution)/shard_map/ppermute | solution.py:536
  798.9 1.2 copy-done.8
  800.1 11.7 %join_rows.4.refs_4_ = bf16[90,360,256]{2,1,0:T(8,128)(2,1)} custom-call(s32[1]{0:T(128)} %bitcast.place, bf16[15,360,128]{2,1,0:T(8,128)(2,1)} %get-tuple-element.89.refs_0_, bf16[15,360,128]{2,1,0:T(8,128)(2,1)} %copy-done.4, bf16[15,360,128]{2,1,0:T(8,128)(2,1)} %copy-done.5, bf16[15,360,128]{2,1,0:T(8,128)(2,1)} %copy-done.8, ...), custom_call_target="tpu_custom_call", output_to_operand_aliasing={{}: (5, {})} | custom-call | bytes 11059200 | tf_op jit(solution)/shard_map/join_rows/pallas_call | solution.py:516
  811.8 17.6 %collective-permute-done.12.refs_2_ = bf16[15,360,128]{2,1,0:T(8,128)(2,1)S(1)} collective-permute-done((bf16[15,360,128]{2,1,0:T(8,128)(2,1)}, bf16[15,360,128]{2,1,0:T(8,128)(2,1)S(1)}, u32[]{:S(2)}, u32[]{:S(2)}) %collective-permute-start.12) | collective-permute-done | bytes 1382432 | tf_op jit(solution)/shard_map/ppermute | solution.py:536
  829.4 28.8 %collective-permute-done.13.refs_3_ = bf16[15,360,128]{2,1,0:T(8,128)(2,1)} collective-permute-done((bf16[15,360,128]{2,1,0:T(8,128)(2,1)}, bf16[15,360,128]{2,1,0:T(8,128)(2,1)}, u32[]{:S(2)}, u32[]{:S(2)}) %collective-permute-start.13) | collective-permute-done | bytes 1382432 | tf_op jit(solution)/shard_map/ppermute | solution.py:536
  858.3 11.7 %join_rows.5 = bf16[90,360,256]{2,1,0:T(8,128)(2,1)} custom-call(s32[1]{0:T(128)} %bitcast.place, bf16[15,360,128]{2,1,0:T(8,128)(2,1)} %get-tuple-element.84.refs_0_, bf16[15,360,128]{2,1,0:T(8,128)(2,1)} %copy-done.6, bf16[15,360,128]{2,1,0:T(8,128)(2,1)} %copy-done.7, ...), custom_call_target="tpu_custom_call", output_to_operand_aliasing={{}: (5, {})} | custom-call | bytes 11059200 | tf_op jit(solution)/shard_map/join_rows/pallas_call | solution.py:516
  (87 shorter events, 15.5 us)
Async XLA Ops:
  0.0 16.4 %copy-start.1 = (bf16[48,80,128]{2,1,0:T(8,128)(2,1)S(1)}, bf16[48,80,128]{2,1,0:T(8,128)(2,1)}, u32[]{:S(2)}) copy-start(bf16[48,80,128]{2,1,0:T(8,128)(2,1)} %param.6) | copy-start | bytes 2949124
  0.0 4.9 copy-start.9
  1.3 15.3 %collective-permute-start.1 = (bf16[24,80,128]{2,1,0:T(8,128)(2,1)S(1)}, bf16[24,80,128]{2,1,0:T(8,128)(2,1)S(1)}, u32[]{:S(2)}, u32[]{:S(2)}) collective-permute-start(bf16[24,80,128]{2,1,0:T(8,128)(2,1)S(1)} %get-tuple-element.95), channel_id=1, source_target_pairs={{1,0},{2,1},{3,2},{0,3},{5,4},{6,5},{7,6},{4,7},{9,8},{10,9},{11,1... | collective-permute-start | bytes 1474568 | tf_op jit(solution)/shard_map/ppermute | solution.py:28
  3.8 12.6 %collective-permute-start = (bf16[24,80,128]{2,1,0:T(8,128)(2,1)S(1)}, bf16[24,80,128]{2,1,0:T(8,128)(2,1)S(1)}, u32[]{:S(2)}, u32[]{:S(2)}) collective-permute-start(bf16[24,80,128]{2,1,0:T(8,128)(2,1)S(1)} %get-tuple-element.96), channel_id=1, source_target_pairs={{0,1},{1,2},{2,3},{3,0},{4,5},{5,6},{6,7},{7,4},{8,9},{9,10},{10,1... | collective-permute-start | bytes 1474568 | tf_op jit(solution)/shard_map/ppermute | solution.py:26
  16.7 1.3 copy-start
  38.9 38.7 %collective-permute-start.2 = (bf16[15,360,128]{2,1,0:T(8,128)(2,1)}, bf16[15,360,128]{2,1,0:T(8,128)(2,1)}, u32[]{:S(2)}, u32[]{:S(2)}) collective-permute-start(bf16[15,360,128]{2,1,0:T(8,128)(2,1)} %get-tuple-element.50), channel_id=1, source_target_pairs={{0,1},{1,0},{2,3},{3,2},{4,5},{5,4},{6,7},{7,6},{8,9},{9,8},{10,11... | collective-permute-start | bytes 4147208 | tf_op jit(solution)/shard_map/ppermute | solution.py:536
  39.0 38.6 %collective-permute-start.3 = (bf16[15,360,128]{2,1,0:T(8,128)(2,1)}, bf16[15,360,128]{2,1,0:T(8,128)(2,1)}, u32[]{:S(2)}, u32[]{:S(2)}) collective-permute-start(bf16[15,360,128]{2,1,0:T(8,128)(2,1)} %get-tuple-element.51), channel_id=1, source_target_pairs={{0,2},{1,3},{2,0},{3,1},{4,6},{5,7},{6,4},{7,5},{8,10},{9,11},{10,... | collective-permute-start | bytes 4147208 | tf_op jit(solution)/shard_map/ppermute | solution.py:536
  40.5 60.7 %collective-permute-start.4 = (bf16[15,360,128]{2,1,0:T(8,128)(2,1)}, bf16[15,360,128]{2,1,0:T(8,128)(2,1)}, u32[]{:S(2)}, u32[]{:S(2)}) collective-permute-start(bf16[15,360,128]{2,1,0:T(8,128)(2,1)} %get-tuple-element.52), channel_id=1, source_target_pairs={{0,3},{1,2},{2,1},{3,0},{4,7},{5,6},{6,5},{7,4},{8,11},{9,10},{10,... | collective-permute-start | bytes 4147208 | tf_op jit(solution)/shard_map/ppermute | solution.py:536
  112.8 79.6 %all-to-all-start = ((bf16[8,30,48,128]{3,2,1,0:T(8,128)(2,1)}), bf16[8,30,48,128]{3,2,1,0:T(8,128)(2,1)S(1)}, u32[]{:S(2)}, u32[]{:S(2)}) async-start(bf16[8,30,48,128]{3,2,1,0:T(8,128)(2,1)} %forward_rows.3), calls=%async_computation | async-start | bytes 5898240 | tf_op jit(solution)/shard_map/all_to_all | solution.py:542
  118.6 23.7 %collective-permute-start.5 = (bf16[15,360,128]{2,1,0:T(8,128)(2,1)}, bf16[15,360,128]{2,1,0:T(8,128)(2,1)}, u32[]{:S(2)}, u32[]{:S(2)}) collective-permute-start(bf16[15,360,128]{2,1,0:T(8,128)(2,1)} %get-tuple-element.62), channel_id=1, source_target_pairs={{0,1},{1,0},{2,3},{3,2},{4,5},{5,4},{6,7},{7,6},{8,9},{9,8},{10,11... | collective-permute-start | bytes 4147208 | tf_op jit(solution)/shard_map/ppermute | solution.py:536
  118.6 33.5 %collective-permute-start.6 = (bf16[15,360,128]{2,1,0:T(8,128)(2,1)}, bf16[15,360,128]{2,1,0:T(8,128)(2,1)}, u32[]{:S(2)}, u32[]{:S(2)}) collective-permute-start(bf16[15,360,128]{2,1,0:T(8,128)(2,1)} %get-tuple-element.63), channel_id=1, source_target_pairs={{0,2},{1,3},{2,0},{3,1},{4,6},{5,7},{6,4},{7,5},{8,10},{9,11},{10,... | collective-permute-start | bytes 4147208 | tf_op jit(solution)/shard_map/ppermute | solution.py:536
  120.2 60.6 %collective-permute-start.7 = (bf16[15,360,128]{2,1,0:T(8,128)(2,1)}, bf16[15,360,128]{2,1,0:T(8,128)(2,1)}, u32[]{:S(2)}, u32[]{:S(2)}) collective-permute-start(bf16[15,360,128]{2,1,0:T(8,128)(2,1)} %get-tuple-element.64), channel_id=1, source_target_pairs={{0,3},{1,2},{2,1},{3,0},{4,7},{5,6},{6,5},{7,4},{8,11},{9,10},{10,... | collective-permute-start | bytes 4147208 | tf_op jit(solution)/shard_map/ppermute | solution.py:536
  192.4 79.8 %all-to-all-start.1 = ((bf16[8,30,48,128]{3,2,1,0:T(8,128)(2,1)}), bf16[8,30,48,128]{3,2,1,0:T(8,128)(2,1)}, u32[]{:S(2)}, u32[]{:S(2)}) async-start(bf16[8,30,48,128]{3,2,1,0:T(8,128)(2,1)} %forward_rows.4), calls=%async_computation.1 | async-start | bytes 5898240 | tf_op jit(solution)/shard_map/all_to_all | solution.py:542
  198.5 3.5 collective-permute-start.8
  198.6 33.5 %collective-permute-start.9 = (bf16[15,360,128]{2,1,0:T(8,128)(2,1)}, bf16[15,360,128]{2,1,0:T(8,128)(2,1)}, u32[]{:S(2)}, u32[]{:S(2)}) collective-permute-start(bf16[15,360,128]{2,1,0:T(8,128)(2,1)} %get-tuple-element.75), channel_id=1, source_target_pairs={{0,2},{1,3},{2,0},{3,1},{4,6},{5,7},{6,4},{7,5},{8,10},{9,11},{10,... | collective-permute-start | bytes 4147208 | tf_op jit(solution)/shard_map/ppermute | solution.py:536
  200.1 60.5 %collective-permute-start.10 = (bf16[15,360,128]{2,1,0:T(8,128)(2,1)}, bf16[15,360,128]{2,1,0:T(8,128)(2,1)}, u32[]{:S(2)}, u32[]{:S(2)}) collective-permute-start(bf16[15,360,128]{2,1,0:T(8,128)(2,1)} %get-tuple-element.76), channel_id=1, source_target_pairs={{0,3},{1,2},{2,1},{3,0},{4,7},{5,6},{6,5},{7,4},{8,11},{9,10},{10,... | collective-permute-start | bytes 4147208 | tf_op jit(solution)/shard_map/ppermute | solution.py:536
  272.2 73.5 %all-to-all-start.2 = ((bf16[8,30,48,128]{3,2,1,0:T(8,128)(2,1)}), bf16[8,30,48,128]{3,2,1,0:T(8,128)(2,1)}, u32[]{:S(2)}, u32[]{:S(2)}) async-start(bf16[8,30,48,128]{3,2,1,0:T(8,128)(2,1)} %forward_rows.5), calls=%async_computation.2 | async-start | bytes 5898240 | tf_op jit(solution)/shard_map/all_to_all | solution.py:542
  529.6 70.0 %all-to-all-start.5 = ((bf16[8,30,48,128]{3,2,1,0:T(8,128)(2,1)}), bf16[8,30,48,128]{3,2,1,0:T(8,128)(2,1)S(1)}, u32[]{:S(2)}, u32[]{:S(2)}) async-start(bf16[8,30,48,128]{3,2,1,0:T(8,128)(2,1)} %bitcast.22), calls=%async_computation.5 | async-start | bytes 5898240 | tf_op jit(solution)/shard_map/all_to_all | solution.py:542
  599.5 1.6 copy-start.3
  601.1 70.3 %all-to-all-start.7 = ((bf16[8,30,48,128]{3,2,1,0:T(8,128)(2,1)}), bf16[8,30,48,128]{3,2,1,0:T(8,128)(2,1)S(1)}, u32[]{:S(2)}, u32[]{:S(2)}) async-start(bf16[8,30,48,128]{3,2,1,0:T(8,128)(2,1)} %bitcast.24), calls=%async_computation.7 | async-start | bytes 5898240 | tf_op jit(solution)/shard_map/all_to_all | solution.py:542
  671.4 1.6 copy-start.2
  673.0 70.4 %all-to-all-start.6 = ((bf16[8,30,48,128]{3,2,1,0:T(8,128)(2,1)}), bf16[8,30,48,128]{3,2,1,0:T(8,128)(2,1)}, u32[]{:S(2)}, u32[]{:S(2)}) async-start(bf16[8,30,48,128]{3,2,1,0:T(8,128)(2,1)} %bitcast.20), calls=%async_computation.6 | async-start | bytes 5898240 | tf_op jit(solution)/shard_map/all_to_all | solution.py:542
  677.5 75.8 %collective-permute-start.17 = (bf16[15,360,128]{2,1,0:T(8,128)(2,1)}, bf16[15,360,128]{2,1,0:T(8,128)(2,1)}, u32[]{:S(2)}, u32[]{:S(2)}) collective-permute-start(bf16[15,360,128]{2,1,0:T(8,128)(2,1)} %get-tuple-element.80), channel_id=1, source_target_pairs={{0,1},{1,0},{2,3},{3,2},{4,5},{5,4},{6,7},{7,6},{8,9},{9,8},{10,11... | collective-permute-start | bytes 4147208 | tf_op jit(solution)/shard_map/ppermute | solution.py:536
  677.6 75.7 %collective-permute-start.18 = (bf16[15,360,128]{2,1,0:T(8,128)(2,1)}, bf16[15,360,128]{2,1,0:T(8,128)(2,1)}, u32[]{:S(2)}, u32[]{:S(2)}) collective-permute-start(bf16[15,360,128]{2,1,0:T(8,128)(2,1)} %get-tuple-element.81), channel_id=1, source_target_pairs={{0,2},{1,3},{2,0},{3,1},{4,6},{5,7},{6,4},{7,5},{8,10},{9,11},{10,... | collective-permute-start | bytes 4147208 | tf_op jit(solution)/shard_map/ppermute | solution.py:536
  678.0 75.8 %collective-permute-start.19 = (bf16[15,360,128]{2,1,0:T(8,128)(2,1)}, bf16[15,360,128]{2,1,0:T(8,128)(2,1)}, u32[]{:S(2)}, u32[]{:S(2)}) collective-permute-start(bf16[15,360,128]{2,1,0:T(8,128)(2,1)} %get-tuple-element.82), channel_id=1, source_target_pairs={{0,3},{1,2},{2,1},{3,0},{4,7},{5,6},{6,5},{7,4},{8,11},{9,10},{10,... | collective-permute-start | bytes 4147208 | tf_op jit(solution)/shard_map/ppermute | solution.py:536
  689.2 66.2 %collective-permute-start.14 = (bf16[15,360,128]{2,1,0:T(8,128)(2,1)}, bf16[15,360,128]{2,1,0:T(8,128)(2,1)S(1)}, u32[]{:S(2)}, u32[]{:S(2)}) collective-permute-start(bf16[15,360,128]{2,1,0:T(8,128)(2,1)} %get-tuple-element.90), channel_id=1, source_target_pairs={{0,1},{1,0},{2,3},{3,2},{4,5},{5,4},{6,7},{7,6},{8,9},{9,8},{10,11... | collective-permute-start | bytes 4147208 | tf_op jit(solution)/shard_map/ppermute | solution.py:536
  689.5 80.7 %collective-permute-start.15 = (bf16[15,360,128]{2,1,0:T(8,128)(2,1)}, bf16[15,360,128]{2,1,0:T(8,128)(2,1)S(1)}, u32[]{:S(2)}, u32[]{:S(2)}) collective-permute-start(bf16[15,360,128]{2,1,0:T(8,128)(2,1)} %get-tuple-element.91), channel_id=1, source_target_pairs={{0,2},{1,3},{2,0},{3,1},{4,6},{5,7},{6,4},{7,5},{8,10},{9,11},{10,... | collective-permute-start | bytes 4147208 | tf_op jit(solution)/shard_map/ppermute | solution.py:536
  753.3 45.7 %collective-permute-start.16 = (bf16[15,360,128]{2,1,0:T(8,128)(2,1)}, bf16[15,360,128]{2,1,0:T(8,128)(2,1)S(1)}, u32[]{:S(2)}, u32[]{:S(2)}) collective-permute-start(bf16[15,360,128]{2,1,0:T(8,128)(2,1)} %get-tuple-element.92), channel_id=1, source_target_pairs={{0,3},{1,2},{2,1},{3,0},{4,7},{5,6},{6,5},{7,4},{8,11},{9,10},{10,... | collective-permute-start | bytes 4147208 | tf_op jit(solution)/shard_map/ppermute | solution.py:536
  753.3 58.5 %collective-permute-start.11 = (bf16[15,360,128]{2,1,0:T(8,128)(2,1)}, bf16[15,360,128]{2,1,0:T(8,128)(2,1)S(1)}, u32[]{:S(2)}, u32[]{:S(2)}) collective-permute-start(bf16[15,360,128]{2,1,0:T(8,128)(2,1)} %get-tuple-element.85), channel_id=1, source_target_pairs={{0,1},{1,0},{2,3},{3,2},{4,5},{5,4},{6,7},{7,6},{8,9},{9,8},{10,11... | collective-permute-start | bytes 4147208 | tf_op jit(solution)/shard_map/ppermute | solution.py:536
  753.7 75.7 %collective-permute-start.12 = (bf16[15,360,128]{2,1,0:T(8,128)(2,1)}, bf16[15,360,128]{2,1,0:T(8,128)(2,1)S(1)}, u32[]{:S(2)}, u32[]{:S(2)}) collective-permute-start(bf16[15,360,128]{2,1,0:T(8,128)(2,1)} %get-tuple-element.86), channel_id=1, source_target_pairs={{0,2},{1,3},{2,0},{3,1},{4,6},{5,7},{6,4},{7,5},{8,10},{9,11},{10,... | collective-permute-start | bytes 4147208 | tf_op jit(solution)/shard_map/ppermute | solution.py:536
  755.4 12.2 %copy-start.4 = (bf16[15,360,128]{2,1,0:T(8,128)(2,1)}, bf16[15,360,128]{2,1,0:T(8,128)(2,1)S(1)}, u32[]{:S(2)}) copy-start(bf16[15,360,128]{2,1,0:T(8,128)(2,1)S(1)} %collective-permute-done.14.refs_1_) | copy-start | bytes 4147204
  755.4 102.9 %collective-permute-start.13 = (bf16[15,360,128]{2,1,0:T(8,128)(2,1)}, bf16[15,360,128]{2,1,0:T(8,128)(2,1)}, u32[]{:S(2)}, u32[]{:S(2)}) collective-permute-start(bf16[15,360,128]{2,1,0:T(8,128)(2,1)} %get-tuple-element.87), channel_id=1, source_target_pairs={{0,3},{1,2},{2,1},{3,0},{4,7},{5,6},{6,5},{7,4},{8,11},{9,10},{10,... | collective-permute-start | bytes 4147208 | tf_op jit(solution)/shard_map/ppermute | solution.py:536
  770.2 28.7 %copy-start.5 = (bf16[15,360,128]{2,1,0:T(8,128)(2,1)}, bf16[15,360,128]{2,1,0:T(8,128)(2,1)S(1)}, u32[]{:S(2)}) copy-start(bf16[15,360,128]{2,1,0:T(8,128)(2,1)S(1)} %collective-permute-done.15.refs_2_) | copy-start | bytes 4147204
  798.9 1.2 copy-start.8
  811.8 46.5 %copy-start.6 = (bf16[15,360,128]{2,1,0:T(8,128)(2,1)}, bf16[15,360,128]{2,1,0:T(8,128)(2,1)S(1)}, u32[]{:S(2)}) copy-start(bf16[15,360,128]{2,1,0:T(8,128)(2,1)S(1)} %collective-permute-done.11.refs_1_) | copy-start | bytes 4147204
  829.4 28.8 %copy-start.7 = (bf16[15,360,128]{2,1,0:T(8,128)(2,1)}, bf16[15,360,128]{2,1,0:T(8,128)(2,1)S(1)}, u32[]{:S(2)}) copy-start(bf16[15,360,128]{2,1,0:T(8,128)(2,1)S(1)} %collective-permute-done.12.refs_2_) | copy-start | bytes 4147204
